TPU v7x, 256 devices: a whole 4x4x8 slice. The times are simulated.
256 devices in a mesh: seq: 64 (over z, x, core), head: 4 (over y).
Axes of the slice: x: 4, y: 4, z: 8, core: 2. Of those that a mesh axis runs over, the one named last changes fastest.
Arguments:
- queries: bfloat16 [32768, 4096], P('seq', 'head'), may hold values from -15 to 15
- keys: bfloat16 [32768, 4096], P('seq', 'head'), may hold values from -15 to 15
- values: bfloat16 [32768, 4096], P('seq', 'head'), may hold values from -6 to 6
- offsets_b: int32 [8, 32], P(None, 'head'), may hold values from 0 to 3
- offsets_c: int32 [32], P('head'), may hold values from 0 to 31
- out_weight: bfloat16 [4096, 4096], P(None, 'head'), may hold values from -0.09375 to 0.09375
Outputs:
- mixed: bfloat16 [32768, 4096], P('seq', 'head')
All inputs are finite; a program needn't handle non-finite values.
Results may differ from a plain program's by a relative error of at most 0.0054.
Values may be sent and summed in bfloat16 or wider, within the bound.
A program may use at most 128 MiB of HBM per device.

v0:
```python
import jax
import jax.numpy as jnp
from jax import lax
from jax.sharding import PartitionSpec as P

HEAD_DIM = 128
RATE_B = 4


masked_score = -1e30


def passed_along(block, axis, distance):
    devices = range(lax.axis_size(axis))
    route = [(i - distance, i) for i in devices if i - distance in devices]
    return lax.ppermute(block, axis, route)


def swapped(block, axis, bit):
    count = lax.axis_size(axis)
    route = []
    for low in range(count):
        high = low | 1 << bit
        if high != low and high < count:
            route += [(low, high), (high, low)]
    return lax.ppermute(block, axis, route)


def attend(query_sub, key_sub, value_sub, allowed):
    score_scale = float(query_sub.shape[2]) ** (-0.5)
    scores = (
        jnp.einsum("ihd,jhd->hij", query_sub, key_sub, preferred_element_type=jnp.float32)
        * score_scale
    )
    scores = jnp.where(allowed[None], scores, masked_score)
    row_top = jnp.max(scores, axis=2)
    weights = jnp.exp(scores - row_top[:, :, None])
    weight_sum = jnp.sum(weights, axis=2)
    numerator = jnp.einsum(
        "hij,jhd->ihd", weights.astype(jnp.bfloat16), value_sub, preferred_element_type=jnp.float32
    )
    return (row_top.T, weight_sum.T, numerator)


def select(field, offset, stride):
    grouped = field.reshape(field.shape[0] // stride, stride, field.shape[1], field.shape[2])
    picked = jnp.arange(stride)[:, None] == offset[None, :]
    return jnp.sum(jnp.where(picked[None, :, :, None], grouped, jnp.zeros((), field.dtype)), axis=1)


def spread(row_top, weight_sum, numerator, offset, stride):
    picked = (jnp.arange(stride)[:, None] == offset[None, :])[None]
    row_count = row_top.shape[0]
    heads_here = row_top.shape[1]
    chosen = jnp.broadcast_to(picked, (row_count, stride, heads_here)).reshape(
        row_count * stride, heads_here
    )
    top_full = jnp.where(picked, row_top[:, None, :], 0.0).reshape(row_count * stride, heads_here)
    sum_full = jnp.where(picked, weight_sum[:, None, :], 0.0).reshape(
        row_count * stride, heads_here
    )
    numer_full = jnp.where(picked[..., None], numerator[:, None], 0.0).reshape(
        row_count * stride, heads_here, numerator.shape[2]
    )
    return (chosen, top_full, sum_full, numer_full)


def combine(levels):
    base_top = levels[0][1]
    peak = base_top
    for chosen, row_top, weight_sum, numerator in levels[1:]:
        peak = jnp.maximum(peak, jnp.where(chosen, row_top, base_top))
    numer_total = jnp.zeros(levels[0][3].shape, jnp.float32)
    denom_total = jnp.zeros(base_top.shape, jnp.float32)
    for chosen, row_top, weight_sum, numerator in levels:
        factor = jnp.where(chosen, jnp.exp(jnp.where(chosen, row_top, peak) - peak), 0.0)
        numer_total = numer_total + factor[..., None] * numerator
        denom_total = denom_total + factor * weight_sum
    return (numer_total / denom_total[..., None]).astype(jnp.bfloat16)


def ordered(mine, other_rows, seq_place, level_bit):
    low_half = seq_place // 2**level_bit % 2 == 0
    return tuple(
        (
            jnp.where(
                low_half,
                jnp.concatenate([first_part, second_part], 0),
                jnp.concatenate([second_part, first_part], 0),
            )
            for first_part, second_part in zip(mine, other_rows)
        )
    )


def local_level(query_all, gathered, offset, stride, block_place):
    query_sub = select(query_all, offset, stride)
    row_count = query_sub.shape[0]
    heads_here = query_all.shape[1]
    key_sub = gathered[0].reshape(gathered[0].shape[0], heads_here, query_all.shape[2])
    value_sub = gathered[1].reshape(gathered[1].shape[0], heads_here, query_all.shape[2])
    global_row = block_place * row_count + jnp.arange(row_count)[:, None]
    allowed = jnp.arange(key_sub.shape[0])[None, :] <= global_row
    row_top, weight_sum, numerator = attend(query_sub, key_sub, value_sub, allowed)
    return spread(row_top, weight_sum, numerator, offset, stride)


def shards(queries, keys, values, offsets_b, offsets_c, out_weight):
    tok_rows = queries.shape[0]
    feature_width = queries.shape[1]
    local_heads = feature_width // HEAD_DIM
    seq_count = lax.axis_size("seq")
    seq_place = lax.axis_index("seq")
    top_stride = seq_count // 2

    def heads_view(field):
        return field.reshape(field.shape[0], local_heads, HEAD_DIM)

    query_all = heads_view(queries)
    key_own = heads_view(keys)
    value_own = heads_view(values)
    odd_place = seq_place % 2 == 1
    row_index = jnp.arange(tok_rows)[:, None]
    col_index = jnp.arange(tok_rows)[None, :]
    diag_top, diag_sum, diag_numer = attend(query_all, key_own, value_own, col_index <= row_index)
    level_diag = (jnp.ones(diag_top.shape, jnp.bool_), diag_top, diag_sum, diag_numer)
    full_block = jnp.ones((tok_rows, tok_rows), jnp.bool_)
    mate_keys, mate_values = passed_along((keys, values), "seq", 1)
    cross_top, cross_sum, cross_numer = attend(
        query_all, heads_view(mate_keys), heads_view(mate_values), full_block
    )
    level_cross = (jnp.broadcast_to(odd_place, cross_top.shape), cross_top, cross_sum, cross_numer)
    offset_b = lax.dynamic_index_in_dim(offsets_b, seq_place // 8, 0, keepdims=False)

    def subset_b(field):
        return select(heads_view(field), offset_b, RATE_B).reshape(-1, feature_width)

    gathered = (subset_b(keys), subset_b(values))
    for level_bit in range(3):
        other_rows = swapped((gathered[0], gathered[1]), "seq", level_bit)
        gathered = ordered(gathered, other_rows, seq_place, level_bit)
    level_b = local_level(query_all, gathered, offset_b, RATE_B, seq_place % 8)

    def subset_c(field):
        return select(heads_view(field), offsets_c, top_stride).reshape(-1, feature_width)

    gathered_top = (
        lax.all_gather(subset_c(keys), "seq", axis=0, tiled=True),
        lax.all_gather(subset_c(values), "seq", axis=0, tiled=True),
    )
    level_c = local_level(query_all, gathered_top, offsets_c, top_stride, seq_place)
    attended = combine([level_diag, level_cross, level_b, level_c]).reshape(tok_rows, feature_width)
    mixed = jnp.dot(
        lax.all_gather(attended, "head", axis=1, tiled=True),
        out_weight,
        preferred_element_type=jnp.float32,
    )
    return mixed.astype(jnp.bfloat16)


def solution(mesh):
    placed = (
        P("seq", "head"),
        P("seq", "head"),
        P("seq", "head"),
        P(None, "head"),
        P("head"),
        P(None, "head"),
    )
    return jax.shard_map(
        shards, mesh=mesh, in_specs=placed, out_specs=P("seq", "head"), check_vma=False
    )
```

profile of v0, /device:TPU:1, one launch (start us, length us, event | category | flops | bytes accessed | tf_op | source)
XLA Modules:
  0.0 282.8 jit_solution(13736710039788219619)
XLA Ops:
  6.5 0.8 iota_compare_fusion.3
  7.3 1.6 copy.94
  8.9 0.3 copy.86
  9.2 0.3 copy.85
  9.5 1.4 fusion.42
  10.9 0.6 copy.142
  11.6 4.5 %collective-permute-start.4 = (bf16[512,1024]{1,0:T(8,128)(2,1)}, bf16[512,1024]{1,0:T(8,128)(2,1)}, u32[]{:S(2)}, u32[]{:S(2)}) collective-permute-start(bf16[512,1024]{1,0:T(8,128)(2,1)} %param.8), channel_id=1, source_target_pairs={{0,4},{4,8},{8,12},{12,16},{16,20},{20,24},{24,28},{28,32},{32,36}... | collective-permute-start | bytes 3145736 | tf_op jit(solution)/shard_map/ppermute | solution.py:16
  16.2 2.2 select_reduce_fusion
  18.3 0.8 copy.139
  19.1 0.9 collective-permute-start.5
  20.0 0.7 copy.140
  20.8 2.4 copy.47
  23.2 2.6 collective-permute-start
  25.8 0.6 copy.141
  26.5 0.8 iota_compare_fusion
  27.3 1.3 copy.82
  28.6 2.8 fusion
  31.5 3.8 %fusion.5 = f32[8,512,128]{1,2,0:T(8,128)} fusion(bf16[512,8,128]{0,2,1:T(8,128)(2,1)S(1)} %bitcast.180, f32[8,512,512]{1,2,0:T(8,128)S(1)} %get-tuple-element.21, f32[8,512]{1,0:T(8,128)S(1)} %get-tuple-element.20, pred[512,512]{0,1:T(8,128)(4,1)S(1)} %copy-done.12), kind=kOutput, calls=%fused_computation.9 | convolution fusion | flops 545259520 | bytes 11812864 | tf_op jit(solution)/shard_map/hij,jhd->ihd/dot_general | solution.py:39
  35.3 0.1 iota_compare_fusion.1
  35.8 0.1 copy.55
  35.9 1.4 maximum_select_fusion.9
  37.3 1.0 collective-permute-start.6
  38.3 1.5 maximum_select_fusion.7
  39.8 0.6 collective-permute-start.2
  40.4 0.7 iota_compare_fusion.2
  41.1 1.0 copy.96
  42.1 1.0 copy.88
  43.3 8.3 %collective-permute-done.6 = bf16[256,1024]{1,0:T(8,128)(2,1)S(1)} collective-permute-done((bf16[256,1024]{1,0:T(8,128)(2,1)S(1)}, bf16[256,1024]{1,0:T(8,128)(2,1)S(1)}, u32[]{:S(2)}, u32[]{:S(2)}) %collective-permute-start.6) | collective-permute-done | bytes 524320 | tf_op jit(solution)/shard_map/ppermute | solution.py:26
  51.6 1.6 maximum_select_fusion.5
  53.2 9.1 %collective-permute-done.2 = bf16[256,1024]{1,0:T(8,128)(2,1)S(1)} collective-permute-done((bf16[256,1024]{1,0:T(8,128)(2,1)S(1)}, bf16[256,1024]{1,0:T(8,128)(2,1)S(1)}, u32[]{:S(2)}, u32[]{:S(2)}) %collective-permute-start.2) | collective-permute-done | bytes 524320 | tf_op jit(solution)/shard_map/ppermute | solution.py:26
  62.5 2.7 collective-permute-start.7
  65.2 1.5 maximum_select_fusion.3
  66.6 0.5 collective-permute-start.3
  67.2 0.2 maximum_select_fusion.2
  67.3 0.2 maximum_select_fusion.4
  67.5 2.3 copy.62
  69.8 2.6 multiply_reduce_fusion
  72.4 9.0 %fusion.1 = (f32[8,512]{1,0:T(8,128)}, f32[8,512]{1,0:T(8,128)}) fusion(f32[8,512,512]{1,2,0:T(8,128)S(1)} %get-tuple-element.23, f32[8,512]{1,0:T(8,128)S(1)} %get-tuple-element.22, f32[8,512]{1,0:T(8,128)S(1)} %copy-done.22, f32[8,512,512]{1,2,0:T(8,128)} %copy-done.4, pred[512,512]{0,1:T(8,128)(4,1)S(1)} %copy-done.13), kind=kLoop, calls=%fused_computation.5 | loop fusion | flops 14671872 | bytes 17104896 | tf_op jit(solution)/shard_map/reduce_sum | solution.py:38
  81.4 11.9 %collective-permute-done.7 = bf16[512,1024]{1,0:T(8,128)(2,1)} collective-permute-done((bf16[512,1024]{1,0:T(8,128)(2,1)}, bf16[512,1024]{1,0:T(8,128)(2,1)}, u32[]{:S(2)}, u32[]{:S(2)}) %collective-permute-start.7) | collective-permute-done | bytes 1048608 | tf_op jit(solution)/shard_map/ppermute | solution.py:26
  93.3 1.5 copy.98
  94.7 21.0 %collective-permute-done.3 = bf16[512,1024]{1,0:T(8,128)(2,1)} collective-permute-done((bf16[512,1024]{1,0:T(8,128)(2,1)}, bf16[512,1024]{1,0:T(8,128)(2,1)}, u32[]{:S(2)}, u32[]{:S(2)}) %collective-permute-start.3) | collective-permute-done | bytes 1048608 | tf_op jit(solution)/shard_map/ppermute | solution.py:26
  115.7 1.5 copy.90
  117.2 0.3 maximum_select_fusion.1
  117.6 0.3 maximum_select_fusion
  117.9 0.6 copy-done.14
  118.5 1.3 fusion.15
  119.8 2.0 copy-done.3
  121.7 1.6 fusion.34
  123.3 0.2 copy.68
  123.6 3.3 %fusion.16 = f32[8,128]{1,0:T(8,128)S(1)} fusion(f32[8,128,1024]{2,1,0:T(8,128)} %copy-done.3, f32[8,128]{1,0:T(8,128)S(1)} %get-tuple-element.18, pred[128,1024]{1,0:T(8,128)(4,1)S(1)} %iota_compare_fusion.1), kind=kLoop, calls=%fused_computation.20 | loop fusion | flops 4193280 | bytes 4333568 | tf_op jit(solution)/shard_map/reduce_sum | solution.py:38
  126.9 0.1 copy.74
  127.3 0.1 broadcast_in_dim.268
  127.5 1.9 copy.69
  129.3 2.9 %copy.57 = bf16[1024,1024]{0,1:T(8,128)(2,1)S(1)} copy(bf16[1024,1024]{1,0:T(8,128)(2,1)} %all-gather.4.cloned.1.call-done) | data formatting | bytes 4194304 | tf_op jit(solution)/shard_map/all_gather | solution.py:148
  132.2 0.5 fusion.78
  132.7 0.2 fusion.51
  132.9 70.2 %all-gather.6.cloned.1.call-done = bf16[1024,1024]{1,0:T(8,128)(2,1)} async-done(((bf16[16,1024]{1,0:T(8,128)(2,1)}), bf16[1024,1024]{1,0:T(8,128)(2,1)}) %all-gather.6.cloned.1.call-update) | async-done | bytes 2097168 | tf_op jit(solution)/shard_map/all_gather | solution.py:149
  203.1 2.9 %copy.70 = bf16[1024,1024]{0,1:T(8,128)(2,1)S(1)} copy(bf16[1024,1024]{1,0:T(8,128)(2,1)} %all-gather.6.cloned.1.call-done) | data formatting | bytes 4194304 | tf_op jit(solution)/shard_map/all_gather | solution.py:149
  206.0 0.7 convolution_bitcast_fusion
  207.1 0.1 broadcast_in_dim.272
  207.3 1.8 copy.73
  209.2 8.6 %fusion.30 = bf16[512,8,128]{0,2,1:T(8,128)(2,1)} fusion(f32[512,8,128]{0,2,1:T(8,128)} %copy.73, f32[512,8,128]{0,2,1:T(8,128)} %copy.69, f32[8,512,128]{1,2,0:T(8,128)} %fusion.5, bf16[512,8,128]{0,2,1:T(8,128)(2,1)S(1)} %bitcast.178, f32[8,512,512]{1,2,0:T(8,128)} %copy-done.2, f32[8,512]{1,0:T(8,128)S(1)} %copy-done.18, ...), kind=kOutput, calls=%fused_computation.37 | convolution fusion | flops 548929536 | bytes 16883712 | tf_op jit(solution)/shard_map/hij,jhd->ihd/dot_general | solution.py:39
  217.8 48.3 %all-gather.8.cloned.1.call-done = bf16[512,4096]{0,1:T(8,128)(2,1)} async-done(((bf16[512,1024]{0,1:T(8,128)(2,1)}), bf16[512,4096]{0,1:T(8,128)(2,1)}) %all-gather.8.cloned.1.call-update) | async-done | bytes 4194320 | tf_op jit(solution)/shard_map/all_gather | solution.py:154
  266.1 10.1 %convolution_convert_fusion = bf16[512,1024]{1,0:T(8,128)(2,1)} fusion(bf16[512,4096]{0,1:T(8,128)(2,1)} %all-gather.8.cloned.1.call-done, bf16[4096,1024]{1,0:T(8,128)(2,1)} %param.11), kind=kOutput, calls=%fused_computation.39 | convolution fusion | flops 4295491584 | bytes 13631488 | tf_op jit(solution)/shard_map/dot_general | solution.py:153
  (85 shorter events, 1.7 us)
Async XLA Ops:
  6.5 9.6 %copy-start = (s32[8,8]{1,0:T(8,128)S(1)}, s32[8,8]{1,0:T(8,128)}, u32[]{:S(2)}) copy-start(s32[8,8]{1,0:T(8,128)} %param.9) | copy-start | bytes 772
  6.5 2.3 copy-start.7
  6.5 122.8 %all-gather.4.cloned.1.call-start = ((), (), s32[]{:S(2)}) async-start(), calls=%async_computation | async-start | bytes 2129920 | tf_op jit(solution)/shard_map/all_gather | solution.py:148
  7.3 1.9 copy-start.5
  11.5 191.6 %all-gather.6.cloned.1.call-start = ((), (), s32[]{:S(2)}) async-start(), calls=%async_computation.1 | async-start | bytes 2129920 | tf_op jit(solution)/shard_map/all_gather | solution.py:149
  11.6 55.9 %collective-permute-start.4 = (bf16[512,1024]{1,0:T(8,128)(2,1)}, bf16[512,1024]{1,0:T(8,128)(2,1)}, u32[]{:S(2)}, u32[]{:S(2)}) collective-permute-start(bf16[512,1024]{1,0:T(8,128)(2,1)} %param.8), channel_id=1, source_target_pairs={{0,4},{4,8},{8,12},{12,16},{16,20},{20,24},{24,28},{28,32},{32,36}... | collective-permute-start | bytes 3145736 | tf_op jit(solution)/shard_map/ppermute | solution.py:16
  18.3 2.4 copy-start.10
  18.3 8.9 %copy-start.9 = (bf16[512,1024]{1,0:T(8,128)(2,1)S(1)}, bf16[512,1024]{1,0:T(8,128)(2,1)}, u32[]{:S(2)}) copy-start(bf16[512,1024]{1,0:T(8,128)(2,1)} %param.8) | copy-start | bytes 3145732
  19.1 16.8 %collective-permute-start.5 = (bf16[128,1024]{1,0:T(8,128)(2,1)}, bf16[128,1024]{1,0:T(8,128)(2,1)}, u32[]{:S(2)}, u32[]{:S(2)}) collective-permute-start(bf16[128,1024]{1,0:T(8,128)(2,1)} %bitcast.150), channel_id=1, source_target_pairs={{0,4},{4,0},{8,12},{12,8},{16,20},{20,16},{24,28},{28,24},{32,36},... | collective-permute-start | bytes 786440 | tf_op jit(solution)/shard_map/ppermute | solution.py:26
  20.8 7.8 %copy-start.6 = (bf16[512,1024]{1,0:T(8,128)(2,1)S(1)}, bf16[512,1024]{1,0:T(8,128)(2,1)}, u32[]{:S(2)}) copy-start(bf16[512,1024]{1,0:T(8,128)(2,1)} %param.6) | copy-start | bytes 3145732
  20.8 7.8 %copy-start.8 = (bf16[512,1024]{1,0:T(8,128)(2,1)S(1)}, bf16[512,1024]{1,0:T(8,128)(2,1)}, u32[]{:S(2)}) copy-start(bf16[512,1024]{1,0:T(8,128)(2,1)} %param.7) | copy-start | bytes 3145732
  20.8 17.5 %collective-permute-start.1 = (bf16[128,1024]{1,0:T(8,128)(2,1)}, bf16[128,1024]{1,0:T(8,128)(2,1)}, u32[]{:S(2)}, u32[]{:S(2)}) collective-permute-start(bf16[128,1024]{1,0:T(8,128)(2,1)} %bitcast.151), channel_id=1, source_target_pairs={{0,4},{4,0},{8,12},{12,8},{16,20},{20,16},{24,28},{28,24},{32,36},... | collective-permute-start | bytes 786440 | tf_op jit(solution)/shard_map/ppermute | solution.py:26
  23.2 46.6 %collective-permute-start = (bf16[512,1024]{0,1:T(8,128)(2,1)}, bf16[512,1024]{0,1:T(8,128)(2,1)}, u32[]{:S(2)}, u32[]{:S(2)}) collective-permute-start(bf16[512,1024]{0,1:T(8,128)(2,1)} %copy.47), channel_id=1, source_target_pairs={{0,4},{4,8},{8,12},{12,16},{16,20},{20,24},{24,28},{28,32},{32,36}... | collective-permute-start | bytes 3145736 | tf_op jit(solution)/shard_map/ppermute | solution.py:16
  26.4 239.7 %all-gather.8.cloned.1.call-start = ((), (), s32[]{:S(2)}) async-start(), calls=%async_computation.2 | async-start | bytes 5242880 | tf_op jit(solution)/shard_map/all_gather | solution.py:154
  28.6 2.8 %copy-start.12 = (pred[512,512]{0,1:T(8,128)(4,1)S(1)}, pred[512,512]{0,1:T(8,128)(4,1)}, u32[]{:S(2)}) copy-start(pred[512,512]{0,1:T(8,128)(4,1)} %iota_compare_fusion) | copy-start | bytes 786436
  28.6 2.8 %copy-start.16 = (bf16[512,1024]{0,1:T(8,128)(2,1)S(1)}, bf16[512,1024]{0,1:T(8,128)(2,1)}, u32[]{:S(2)}) copy-start(bf16[512,1024]{0,1:T(8,128)(2,1)} %copy.82) | copy-start | bytes 3145732
  31.4 3.9 %copy-start.4 = (f32[8,512,512]{1,2,0:T(8,128)}, f32[8,512,512]{1,2,0:T(8,128)S(1)}, u32[]{:S(2)}) copy-start(f32[8,512,512]{1,2,0:T(8,128)S(1)} %get-tuple-element.21) | copy-start | bytes 25165828
  31.4 3.9 %copy-start.21 = (f32[8,512]{1,0:T(8,128)}, f32[8,512]{1,0:T(8,128)S(1)}, u32[]{:S(2)}) copy-start(f32[8,512]{1,0:T(8,128)S(1)} %get-tuple-element.20) | copy-start | bytes 49156
  35.3 7.8 %copy-start.11 = (bf16[128,8,128]{2,1,0:T(8,128)(2,1)S(1)}, bf16[128,8,128]{2,1,0:T(8,128)(2,1)}, u32[]{:S(2)}) copy-start(bf16[128,8,128]{2,1,0:T(8,128)(2,1)} %copy-done.10) | copy-start | bytes 786436
  37.3 14.3 %collective-permute-start.6 = (bf16[256,1024]{1,0:T(8,128)(2,1)S(1)}, bf16[256,1024]{1,0:T(8,128)(2,1)S(1)}, u32[]{:S(2)}, u32[]{:S(2)}) collective-permute-start(bf16[256,1024]{1,0:T(8,128)(2,1)S(1)} %maximum_select_fusion.9), channel_id=1, source_target_pairs={{0,8},{8,0},{4,12},{12,4},{16,24},{24,16},{20,28},{28,20},{32,40},... | collective-permute-start | bytes 1572872 | tf_op jit(solution)/shard_map/ppermute | solution.py:26
  39.8 22.5 %collective-permute-start.2 = (bf16[256,1024]{1,0:T(8,128)(2,1)S(1)}, bf16[256,1024]{1,0:T(8,128)(2,1)S(1)}, u32[]{:S(2)}, u32[]{:S(2)}) collective-permute-start(bf16[256,1024]{1,0:T(8,128)(2,1)S(1)} %maximum_select_fusion.7), channel_id=1, source_target_pairs={{0,8},{8,0},{4,12},{12,4},{16,24},{24,16},{20,28},{28,20},{32,40},... | collective-permute-start | bytes 1572872 | tf_op jit(solution)/shard_map/ppermute | solution.py:26
  62.5 30.8 %collective-permute-start.7 = (bf16[512,1024]{1,0:T(8,128)(2,1)}, bf16[512,1024]{1,0:T(8,128)(2,1)}, u32[]{:S(2)}, u32[]{:S(2)}) collective-permute-start(bf16[512,1024]{1,0:T(8,128)(2,1)} %maximum_select_fusion.5), channel_id=1, source_target_pairs={{0,16},{16,0},{4,20},{20,4},{8,24},{24,8},{12,28},{28,12},{32,48},... | collective-permute-start | bytes 3145736 | tf_op jit(solution)/shard_map/ppermute | solution.py:26
  66.6 49.1 %collective-permute-start.3 = (bf16[512,1024]{1,0:T(8,128)(2,1)}, bf16[512,1024]{1,0:T(8,128)(2,1)}, u32[]{:S(2)}, u32[]{:S(2)}) collective-permute-start(bf16[512,1024]{1,0:T(8,128)(2,1)} %maximum_select_fusion.3), channel_id=1, source_target_pairs={{0,16},{16,0},{4,20},{20,4},{8,24},{24,8},{12,28},{28,12},{32,48},... | collective-permute-start | bytes 3145736 | tf_op jit(solution)/shard_map/ppermute | solution.py:26
  69.8 2.6 copy-start.13
  69.8 2.6 copy-start.22
  72.4 9.0 %copy-start.2 = (f32[8,512,512]{1,2,0:T(8,128)}, f32[8,512,512]{1,2,0:T(8,128)S(1)}, u32[]{:S(2)}) copy-start(f32[8,512,512]{1,2,0:T(8,128)S(1)} %get-tuple-element.23) | copy-start | bytes 25165828
  72.4 9.0 %copy-start.17 = (f32[8,512]{1,0:T(8,128)}, f32[8,512]{1,0:T(8,128)S(1)}, u32[]{:S(2)}) copy-start(f32[8,512]{1,0:T(8,128)S(1)} %get-tuple-element.22) | copy-start | bytes 49156
  117.6 1.0 copy-start.14
  119.8 2.0 copy-start.3
  129.3 2.9 %copy-start.19 = (bf16[16,8,128]{2,1,0:T(8,128)(2,1)S(1)}, bf16[16,8,128]{2,1,0:T(8,128)(2,1)}, u32[]{:S(2)}) copy-start(bf16[16,8,128]{2,1,0:T(8,128)(2,1)} %get-tuple-element.5) | copy-start | bytes 98308
  129.3 2.9 %copy-start.20 = (pred[16,1024]{1,0:T(8,128)(4,1)S(1)}, pred[16,1024]{1,0:T(8,128)(4,1)}, u32[]{:S(2)}) copy-start(pred[16,1024]{1,0:T(8,128)(4,1)} %iota_compare_fusion.2) | copy-start | bytes 49156
  207.2 1.9 copy-start.18
  207.2 1.9 copy-start.23
  207.3 1.9 copy-start.24
  207.3 1.9 copy-start.25
  207.3 1.9 copy-start.15
  266.1 10.1 %copy-start.1 = (s32[8,8]{1,0:T(8,128)S(1)}, s32[8,8]{1,0:T(8,128)}, u32[]{:S(2)}) copy-start(s32[8,8]{1,0:T(8,128)} %param.9) | copy-start | bytes 772
Sparse Core Ops, SparseCore 0:
  11.6 111.0 all-gather.3
  125.5 77.6 all-gather.5
  217.9 48.1 all-gather.7
where the time goes:
time: 283 us
  waiting for transfers between devices  169 us (60%)
  matrix products  31.9 us (11%)
  local copies, waits for them, and re-layouts  29.9 us (11%)
  other arithmetic  25.5 us (9%)
  between operations  13.7 us (5%)
  starting transfers between devices  13 us (5%)
    all_gather x1, waiting for transfers between devices, shards(): lax.all_gather(subset_c(values), 'seq', axis=0, tiled=True)  70.2 us
    ppermute x6, waiting for transfers between devices, swapped(): return lax.ppermute(block, axis, route)  50.2 us
    all_gather x1, waiting for transfers between devices, shards(): lax.all_gather(attended, 'head', axis=1, tiled=True)  48.3 us
    unnamed x66, local copies, waits for them, and re-layouts  15.1 us
    dot_general x4, matrix products, attend(): jnp.einsum('hij,jhd->ihd', weights.astype(jnp.bfloat16), value_sub, prefe...  14.7 us
    reduce_sum x3, other arithmetic, attend(): weight_sum = jnp.sum(weights, axis=2)  12.5 us
    dot_general x1, matrix products, shards(): jnp.dot(lax.all_gather(attended, 'head', axis=1, tiled=True), out_weight,...  10.1 us
    ppermute x2, starting transfers between devices, passed_along(): return lax.ppermute(block, axis, route)  7.09 us
  transfers between devices with their start and end apart: 11, of which 6 were waited for; matrix products, arithmetic and copies ran while one was open for 19% of the time, Pallas kernels for 0%

commit v1 on v0

v1 whole, which is shorter than its diff:
```python
import functools

import jax
import jax.numpy as jnp
from jax import lax
from jax.experimental import pallas as pl
from jax.experimental.pallas import tpu as pltpu
from jax.sharding import PartitionSpec as P

HEAD_DIM = 128
RATE_B = 4
LOG2E = 1.4426950408889634
NEG = -1e30
MESH = pl.DeviceIdType.MESH
F32 = jnp.float32
BF16 = jnp.bfloat16
NN = (((1,), (0,)), ((), ()))
NT = (((1,), (1,)), ((), ()))
TN = (((0,), (0,)), ((), ()))


def dot(a, b, dims=NN):
    return lax.dot_general(a, b, dims, preferred_element_type=F32)


def iota(shape, axis):
    return lax.broadcasted_iota(jnp.int32, shape, axis)


def one_hot(shape, condition):
    return jnp.where(condition, jnp.ones(shape, F32), jnp.zeros(shape, F32)).astype(BF16)


def late_other(b, c):
    residue = lax.rem(c, RATE_B)
    return jnp.where(residue == b, lax.rem(b + 1, RATE_B), residue)


def stat_rows(count, level):
    high = level.astype(BF16).astype(F32)
    rest = level - high
    mid = rest.astype(BF16).astype(F32)
    low = rest - mid
    row = iota((count, level.shape[1]), 0)
    zero = jnp.zeros((count, level.shape[1]), F32)
    return jnp.where(row == 0, high, jnp.where(row == 1, mid, jnp.where(row == 2, low, zero)))


def kernel(
    q_hbm, k_hbm, v_hbm, offs_b, offs_c, w_hbm, out_hbm,
    qv, kv, vv, mkv, wv, st1b, st1c, rc1b, rc1c, ckv, pm, pmt, oa, la,
    rbst, rbrc, rcst, rcrc, xs, xr, att, acc, outv, ost, orc, osm,
    ld_s, mate_ss, mate_rs, p1c_ss, p1c_rs, p1b_ss, p1b_rs, zg_ss, zg_rs,
    rb_ss, rb_rs, rc_ss, rc_rs, x_ss, x_rs, f_ss, of_ss, of_rs, os_s, out_s,
):
    rows, width = qv.shape
    heads = width // HEAD_DIM
    half = rows // 2
    sel_b = rows // RATE_B
    sel_c = st1c.shape[1]
    top_stride = rows // sel_c
    scale = HEAD_DIM**-0.5 * LOG2E

    s = lax.axis_index("seq")
    y = lax.axis_index("head")
    ny = lax.axis_size("head")
    nz = lax.axis_size("seq") // heads
    z = s // heads
    i = s % heads
    core = s % 2
    right = (y + 1) % ny
    left = (y + ny - 1) % ny

    def plane(j):
        return {"seq": z * heads + j}

    def along_z(t):
        return {"seq": t * heads + i}

    def remote(src, dst, ssem, rsem, device):
        return pltpu.make_async_remote_copy(
            src_ref=src, dst_ref=dst, send_sem=ssem, recv_sem=rsem, device_id=device, device_id_type=MESH
        )

    loads = [
        pltpu.make_async_copy(src, dst, ld_s.at[n])
        for n, (src, dst) in enumerate(((q_hbm, qv), (k_hbm, kv), (v_hbm, vv), (w_hbm, wv)))
    ]
    for copy in loads:
        copy.start()
    barrier = pltpu.get_barrier_semaphore()

    def greet_plane(d, _):
        pl.semaphore_signal(barrier, 1, device_id=plane((i + d) % heads), device_id_type=MESH)
        return 0

    def greet_z(d, _):
        pl.semaphore_signal(barrier, 1, device_id=along_z((z + d) % nz), device_id_type=MESH)
        return 0

    lax.fori_loop(1, heads, greet_plane, 0)
    lax.fori_loop(1, nz, greet_z, 0)
    for d in range(1, 4):
        pl.semaphore_signal(barrier, 1, device_id={"head": (y + d) % ny}, device_id_type=MESH)

    for r in range(RATE_B):
        pm[r] = one_hot((sel_b, rows), iota((sel_b, rows), 1) == RATE_B * iota((sel_b, rows), 0) + r)
    for r in range(RATE_B):
        pmt[:, r * sel_b : (r + 1) * sel_b] = one_hot(
            (rows, sel_b), iota((rows, sel_b), 0) == RATE_B * iota((rows, sel_b), 1) + r
        )
    table = jnp.zeros((heads, 128), jnp.int32)
    for h in range(heads):
        b = offs_b[z, h]
        c = late_other(b, offs_c[0, h])
        pair = jnp.where(iota((heads, 128), 1) == 0, b, c)
        table = jnp.where(iota((heads, 128), 0) == h, pair, table)
    ost[...] = table
    own_table = pltpu.make_async_copy(ost, osm.at[0], os_s.at[0])
    own_table.start()

    pl.semaphore_wait(barrier, (heads - 1) + (nz - 1) + 3)

    def mate_copy(n, device):
        src = (k_hbm, v_hbm)[n]
        return remote(src, mkv.at[n], mate_ss.at[n], mate_rs.at[n], device)

    @pl.when(core == 0)
    def _():
        for n in range(2):
            mate_copy(n, plane(i + 1)).start()

    def table_copy(d):
        return remote(ost, orc.at[d - 1], of_ss.at[d - 1], of_rs.at[d - 1], {"head": (y + d) % ny})

    for d in range(1, 4):
        table_copy(d).start()

    for copy in loads[:3]:
        copy.wait()

    def p1c(j, src):
        return remote(st1c.at[j], rc1c.at[src], p1c_ss.at[j], p1c_rs.at[src], plane(j))

    def p1b(j, src):
        return remote(st1b.at[j], rc1b.at[src], p1b_ss.at[j], p1b_rs.at[src], plane(j))

    def pick(d, _):
        j = (i + 1 + d) % heads
        b = offs_b[z, j]
        c = offs_c[0, j]
        cols = pl.ds(pl.multiple_of(j * HEAD_DIM, HEAD_DIM), HEAD_DIM)
        shape = (sel_b + sel_c, rows)
        row = iota(shape, 0)
        at = jnp.where(row < sel_b, RATE_B * row + b, top_stride * (row - sel_b) + c)
        chosen = one_hot(shape, iota(shape, 1) == at)
        for n, field in enumerate((qv, kv, vv)):
            found = dot(chosen, field[:, cols]).astype(BF16)
            st1b[j, :, n * HEAD_DIM : (n + 1) * HEAD_DIM] = found[:sel_b]
            st1c[j, :, n * HEAD_DIM : (n + 1) * HEAD_DIM] = found[sel_b:]

        @pl.when(j != i)
        def _():
            p1c(j, i).start()

        return 0

    lax.fori_loop(0, heads, pick, 0)

    def send_b(d, _):
        p1b((i + d) % heads, i).start()
        return 0

    lax.fori_loop(1, heads, send_b, 0)
    rc1b[i] = st1b[i]
    rc1c[i] = st1c[i]

    def x_send(h, part, to_right):
        n = 0 if to_right else 1
        slot = 0 if to_right else 2
        device = {"head": right if to_right else left}
        return remote(xs.at[h, part], xr.at[slot, h, part], x_ss.at[n, h, part], x_rs.at[slot, h, part], device)

    def x_recv(slot, h, part):
        return remote(xs.at[h, part], xr.at[slot, h, part], f_ss.at[h, part], x_rs.at[slot, h, part], {"head": right})

    def x_forward(h, part, to_right):
        device = {"head": right if to_right else left}
        return remote(
            xr.at[0 if to_right else 2, h, part], xr.at[1, h, part], f_ss.at[h, part], x_rs.at[1, h, part], device
        )

    def forward(h, part):
        x_recv(0, h, part).wait_recv()
        x_recv(2, h, part).wait_recv()

        @pl.when(h % 2 == 0)
        def _():
            x_forward(h, part, True).start()

        @pl.when(h % 2 == 1)
        def _():
            x_forward(h, part, False).start()

    def attend(key_parts, value_parts, query):
        scores = []
        for keys, allowed in key_parts:
            part = dot(keys, query, NT) * scale
            scores.append(part if allowed is None else jnp.where(allowed, part, NEG))
        top = functools.reduce(jnp.maximum, [jnp.max(part, axis=0, keepdims=True) for part in scores])
        weights = [jnp.exp2(part - top) for part in scores]
        total = functools.reduce(jnp.add, [jnp.sum(part, axis=0, keepdims=True) for part in weights])
        numer = functools.reduce(
            jnp.add, [dot(values, part.astype(BF16), TN) for values, part in zip(value_parts, weights)]
        )
        return numer / total, top + jnp.log2(total)

    def lowest(h, with_mate):
        cols = pl.ds(pl.multiple_of(h * HEAD_DIM, HEAD_DIM), HEAD_DIM)
        causal = iota((half, half), 0) <= iota((half, half), 1)
        for n in range(2):
            key_parts = [(kv[n * half : (n + 1) * half, cols], causal)]
            value_parts = [vv[n * half : (n + 1) * half, cols]]
            if n:
                key_parts.append((kv[:half, cols], None))
                value_parts.append(vv[:half, cols])
            if with_mate:
                key_parts.append((mkv[0, :, cols], None))
                value_parts.append(mkv[1, :, cols])
            out, level = attend(key_parts, value_parts, qv[n * half : (n + 1) * half, cols])
            oa[h, :, n * half : (n + 1) * half] = out
            la[h, :, n * half : (n + 1) * half] = jnp.broadcast_to(level, (8, half))

    @pl.when(core == 1)
    def _():
        for n in range(2):
            mate_copy(n, plane(i - 1)).wait_recv()

    def zg(t, src):
        return remote(ckv.at[src], ckv.at[src], zg_ss.at[t], zg_rs.at[src], along_z(t))

    def lowest_level(h, _):
        @pl.when(core == 1)
        def _():
            lowest(h, True)

        @pl.when(core == 0)
        def _():
            lowest(h, False)

        b = offs_b[z, h]
        c = late_other(b, offs_c[0, h])
        zero_free = jnp.logical_and(b != 0, c != 0)
        one_free = jnp.logical_and(b != 1, c != 1)
        first = jnp.where(zero_free, 0, jnp.where(one_free, 1, 2))
        three_free = jnp.logical_and(b != 3, c != 3)
        two_free = jnp.logical_and(b != 2, c != 2)
        second = jnp.where(three_free, 3, jnp.where(two_free, 2, 1))
        here = oa[h].astype(BF16)
        xs[h, 0, :sel_b] = dot(pm[first], here, NT).astype(BF16)
        xs[h, 0, sel_b:] = dot(pm[second], here, NT).astype(BF16)
        x_send(h, 0, True).start()
        x_send(h, 0, False).start()

        @pl.when(h == 3)
        def _():
            def wait_c(d, _):
                p1c(i, (i + d) % heads).wait_recv()
                return 0

            lax.fori_loop(1, heads, wait_c, 0)
            for j in range(heads):
                ckv[z, j * sel_c : (j + 1) * sel_c, :] = rc1c[j, :, HEAD_DIM:]

            def send_c(d, _):
                zg((z + d) % nz, z).start()
                return 0

            lax.fori_loop(1, nz, send_c, 0)

        return 0

    lax.fori_loop(0, heads, lowest_level, 0)

    def forward_early(h, _):
        forward(h, 0)
        return 0

    lax.fori_loop(0, heads // 2, forward_early, 0)

    def wait_b(d, _):
        p1b(i, (i + d) % heads).wait_recv()
        return 0

    lax.fori_loop(1, heads, wait_b, 0)

    def rb(j, src):
        return remote(rbst.at[j], rbrc.at[src], rb_ss.at[j], rb_rs.at[src], plane(j))

    def rc(j, src):
        return remote(rcst.at[j], rcrc.at[src], rc_ss.at[j], rc_rs.at[src], plane(j))

    def field_b(first, last, n):
        part = rc1b[first:last, :, n * HEAD_DIM : (n + 1) * HEAD_DIM]
        return part.reshape((last - first) * sel_b, HEAD_DIM)

    for pair in range(heads // 2):
        first = 2 * pair
        block = 2 * sel_b
        causal = iota((block, block), 0) <= iota((block, block), 1)
        key_parts = [(field_b(first, first + 2, 1), causal)]
        value_parts = [field_b(first, first + 2, 2)]
        if pair:
            key_parts.append((field_b(0, first, 1), None))
            value_parts.append(field_b(0, first, 2))
        out, level = attend(key_parts, value_parts, field_b(first, first + 2, 0))
        stats = stat_rows(16, level)
        for n in range(2):
            cols = slice(n * sel_b, (n + 1) * sel_b)
            rbst[first + n, :HEAD_DIM] = out[:, cols].astype(BF16)
            rbst[first + n, HEAD_DIM:] = stats[:, cols].astype(BF16)

            @pl.when(first + n != i)
            def _():
                rb(first + n, i).start()

    rbrc[i] = rbst[i]

    lax.fori_loop(heads // 2, heads, forward_early, 0)

    def wait_z(d, _):
        zg(z, (z + d) % nz).wait_recv()
        return 0

    lax.fori_loop(1, nz, wait_z, 0)
    count_c = heads * sel_c
    keys_c = ckv[:, :, :HEAD_DIM].reshape(nz * count_c, HEAD_DIM)
    values_c = ckv[:, :, HEAD_DIM:].reshape(nz * count_c, HEAD_DIM)
    query_c = rc1c[:, :, :HEAD_DIM].reshape(count_c, HEAD_DIM)
    shape_c = (nz * count_c, count_c)
    allowed_c = iota(shape_c, 0) <= iota(shape_c, 1) + z * count_c
    out, level = attend([(keys_c, allowed_c)], [values_c], query_c)
    flat = jnp.concatenate([out.T, stat_rows(HEAD_DIM, level).T], axis=1).astype(BF16)
    rcst[...] = flat.reshape(heads, sel_c, 2 * HEAD_DIM)
    rcrc[i] = rcst[i]

    def send_rc(d, _):
        rc((i + d) % heads, i).start()
        return 0

    lax.fori_loop(1, heads, send_rc, 0)

    def combine(h, _):
        @pl.when(h != i)
        def _():
            rb(i, h).wait_recv()
            rc(i, h).wait_recv()

        b = offs_b[z, h]
        c = offs_c[0, h]
        put_b = one_hot((sel_b, rows), iota((sel_b, rows), 1) == RATE_B * iota((sel_b, rows), 0) + b)
        put_c = one_hot((sel_c, rows), iota((sel_c, rows), 1) == top_stride * iota((sel_c, rows), 0) + c)
        from_b = dot(rbrc[h], put_b)
        from_c = dot(rcrc[h], put_c, TN)

        def level_of(field):
            return jnp.sum(field[HEAD_DIM : HEAD_DIM + 8], axis=0, keepdims=True)

        column = iota((1, rows), 1)
        level_a = la[h, 0:1, :]
        level_b = jnp.where(lax.rem(column, RATE_B) == b, level_of(from_b), NEG)
        level_c = jnp.where(lax.rem(column, top_stride) == c, level_of(from_c), NEG)
        peak = jnp.maximum(level_a, jnp.maximum(level_b, level_c))
        factor_a = jnp.exp2(level_a - peak)
        factor_b = jnp.exp2(level_b - peak)
        factor_c = jnp.exp2(level_c - peak)
        share = 1.0 / (factor_a + factor_b + factor_c)
        whole = (
            (factor_a * share) * oa[h]
            + (factor_b * share) * from_b[:HEAD_DIM]
            + (factor_c * share) * from_c[:HEAD_DIM]
        ).astype(BF16)
        xs[h, 1, :sel_b] = dot(pm[b], whole, NT).astype(BF16)
        xs[h, 1, sel_b:] = dot(pm[late_other(b, c)], whole, NT).astype(BF16)
        x_send(h, 1, True).start()
        x_send(h, 1, False).start()
        return 0

    lax.fori_loop(0, heads, combine, 0)

    own_table.wait()
    for d in range(1, 4):
        table_copy(d).wait_recv()
    tables = [pltpu.make_async_copy(orc.at[d - 1], osm.at[d], os_s.at[d]) for d in range(1, 4)]
    for copy in tables:
        copy.start()
    for copy in tables:
        copy.wait()
    loads[3].wait()

    def place(d, h, early, late):
        b = osm[d, h, 0]
        c = osm[d, h, 1]
        blocks = (early[:sel_b], early[sel_b:], late[:sel_b], late[sel_b:])
        cols = pl.ds(pl.multiple_of(h * HEAD_DIM, HEAD_DIM), HEAD_DIM)
        for r in range(RATE_B):
            at = r - jnp.where(b < r, 1, 0) - jnp.where(c < r, 1, 0)
            mine = lax.select(at == 0, blocks[0], blocks[1])
            mine = lax.select(c == r, blocks[3], mine)
            mine = lax.select(b == r, blocks[2], mine)
            att[d, r * sel_b : (r + 1) * sel_b, cols] = mine

    def place_own(h, _):
        place(0, h, xs[h, 0], xs[h, 1])
        return 0

    lax.fori_loop(0, heads, place_own, 0)
    chunk = 256

    def project(d, first, count, fresh):
        group = (y + ny - d) % ny
        depth = count * HEAD_DIM
        at = pl.multiple_of(group * width + first * HEAD_DIM, HEAD_DIM)
        block = att[d, :, pl.ds(pl.multiple_of(first * HEAD_DIM, HEAD_DIM), depth)]

        def columns(n, _):
            cols = pl.ds(pl.multiple_of(n * chunk, chunk), chunk)
            part = dot(block, wv[pl.ds(at, depth), cols])
            if fresh:
                acc[:, cols] = part
            else:
                acc[:, cols] += part
            return 0

        lax.fori_loop(0, width // chunk, columns, 0)

    project(0, 0, heads, True)

    def opposite(p):
        for n in range(2):
            h = 2 * p + n
            x_recv(1, h, 0).wait_recv()
            x_recv(1, h, 1).wait_recv()
            place(2, h, xr[1, h, 0], xr[1, h, 1])
        project(2, 2 * p, 2, False)

    def remote_pair(p, _):
        for n in range(2):
            forward(2 * p + n, 1)
        for d in (1, 3):
            for n in range(2):
                h = 2 * p + n
                place(d, h, xr[d - 1, h, 0], xr[d - 1, h, 1])
            project(d, 2 * p, 2, False)

        @pl.when(p > 0)
        def _():
            opposite(p - 1)

        return 0

    lax.fori_loop(0, heads // 2, remote_pair, 0)
    opposite(heads // 2 - 1)

    def finish(n, _):
        cols = pl.ds(pl.multiple_of(n * chunk, chunk), chunk)
        outv[:, cols] = dot(pmt[...], acc[:, cols].astype(BF16)).astype(BF16)
        return 0

    lax.fori_loop(0, width // chunk, finish, 0)
    store = pltpu.make_async_copy(outv, out_hbm, out_s)
    store.start()

    @pl.when(core == 0)
    def _():
        for n in range(2):
            mate_copy(n, plane(i + 1)).wait_send()

    for d in range(1, 4):
        table_copy(d).wait_send()

    def sent_plane(d, _):
        j = (i + d) % heads
        p1c(j, i).wait_send()
        p1b(j, i).wait_send()
        rb(j, i).wait_send()
        rc(j, i).wait_send()
        return 0

    lax.fori_loop(1, heads, sent_plane, 0)

    def sent_z(d, _):
        zg((z + d) % nz, z).wait_send()
        return 0

    lax.fori_loop(1, nz, sent_z, 0)

    def sent_y(h, _):
        for part in range(2):
            x_send(h, part, True).wait_send()
            x_send(h, part, False).wait_send()
            x_forward(h, part, True).wait_send()
        return 0

    lax.fori_loop(0, heads, sent_y, 0)
    store.wait()


def shards(queries, keys, values, offsets_b, offsets_c, out_weight):
    rows, width = queries.shape
    depth, features = out_weight.shape
    heads = width // HEAD_DIM
    nz = lax.axis_size("seq") // heads
    ny = lax.axis_size("head")
    sel_b = rows // RATE_B
    sel_c = rows // (lax.axis_size("seq") // 2)
    three = 3 * HEAD_DIM
    dma = pltpu.SemaphoreType.DMA
    hbm = pl.BlockSpec(memory_space=pl.ANY)
    smem = pl.BlockSpec(memory_space=pltpu.SMEM)
    scratch = [
        pltpu.VMEM((rows, width), BF16),
        pltpu.VMEM((rows, width), BF16),
        pltpu.VMEM((rows, width), BF16),
        pltpu.VMEM((2, rows, width), BF16),
        pltpu.VMEM((depth, features), BF16),
        pltpu.VMEM((heads, sel_b, three), BF16),
        pltpu.VMEM((heads, sel_c, three), BF16),
        pltpu.VMEM((heads, sel_b, three), BF16),
        pltpu.VMEM((heads, sel_c, three), BF16),
        pltpu.VMEM((nz, heads * sel_c, 2 * HEAD_DIM), BF16),
        pltpu.VMEM((RATE_B, sel_b, rows), BF16),
        pltpu.VMEM((rows, rows), BF16),
        pltpu.VMEM((heads, HEAD_DIM, rows), F32),
        pltpu.VMEM((heads, 8, rows), F32),
        pltpu.VMEM((heads, HEAD_DIM + 16, sel_b), BF16),
        pltpu.VMEM((heads, HEAD_DIM + 16, sel_b), BF16),
        pltpu.VMEM((heads, sel_c, 2 * HEAD_DIM), BF16),
        pltpu.VMEM((heads, sel_c, 2 * HEAD_DIM), BF16),
        pltpu.VMEM((heads, 2, 2 * sel_b, HEAD_DIM), BF16),
        pltpu.VMEM((3, heads, 2, 2 * sel_b, HEAD_DIM), BF16),
        pltpu.VMEM((ny, rows, width), BF16),
        pltpu.VMEM((rows, features), F32),
        pltpu.VMEM((rows, features), BF16),
        pltpu.VMEM((heads, 128), jnp.int32),
        pltpu.VMEM((3, heads, 128), jnp.int32),
        pltpu.SMEM((ny, heads, 128), jnp.int32),
        dma((4,)),
        dma((2,)),
        dma((2,)),
        dma((heads,)),
        dma((heads,)),
        dma((heads,)),
        dma((heads,)),
        dma((nz,)),
        dma((nz,)),
        dma((heads,)),
        dma((heads,)),
        dma((heads,)),
        dma((heads,)),
        dma((2, heads, 2)),
        dma((3, heads, 2)),
        dma((heads, 2)),
        dma((3,)),
        dma((3,)),
        dma((ny,)),
        dma(()),
    ]
    return pl.pallas_call(
        kernel,
        out_shape=jax.ShapeDtypeStruct((rows, features), BF16),
        in_specs=[hbm, hbm, hbm, smem, smem, hbm],
        out_specs=hbm,
        scratch_shapes=scratch,
        compiler_params=pltpu.CompilerParams(
            collective_id=0, has_side_effects=True, vmem_limit_bytes=56 * 2**20
        ),
    )(queries, keys, values, offsets_b, offsets_c.reshape(1, heads), out_weight)


def solution(mesh):
    placed = (
        P("seq", "head"),
        P("seq", "head"),
        P("seq", "head"),
        P(None, "head"),
        P("head"),
        P(None, "head"),
    )
    return jax.shard_map(
        shards, mesh=mesh, in_specs=placed, out_specs=P("seq", "head"), check_vma=False
    )
```

time: 283 us -> 63 us (0.22)
  the two profiles are of different devices: /device:TPU:1 before, /device:TPU:36 now
where the time goes in v1:
time: 63 us; the launch traced here: 62.9 us
  Pallas kernels  60.6 us (96%)
  local copies, waits for them, and re-layouts  2.26 us (4%)
    pallas_call x1, Pallas kernels, shards(): pl.pallas_call(kernel, out_shape=jax.ShapeDtypeStruct((rows, features), B...  60.6 us
    unnamed x1, local copies, waits for them, and re-layouts  2.26 us

profile of v1, /device:TPU:36, one launch (start us, length us, event | category | flops | bytes accessed | tf_op | source)
XLA Modules:
  0.0 62.9 jit_solution(12808886576390217440)
XLA Ops:
  0.0 60.6 %shard_map.64 = bf16[512,1024]{1,0:T(8,128)(2,1)} custom-call(bf16[512,1024]{1,0:T(8,128)(2,1)} %q_hbm.1, bf16[512,1024]{1,0:T(8,128)(2,1)} %k_hbm.1, bf16[512,1024]{1,0:T(8,128)(2,1)} %v_hbm.1, s32[8,8]{1,0:T(8,128)} %offs_b.1, s32[1,8]{1,0:T(1,128)} %bitcast.1, bf16[4096,1024]{1,0:T(8,128)(2,1)} %w_hbm.1), custom_call_target="tpu_custom_call" | custom-call | tf_op jit(solution)/shard_map/pallas_call | solution.py:569
  60.6 2.3 %copy.8 = bf16[512,1024]{1,0:T(8,128)(2,1)} copy(bf16[512,1024]{1,0:T(8,128)(2,1)} %shard_map.64) | data formatting | bytes 2097152

commit v2 on v1

v2 whole, which is shorter than its diff:
```python
import functools

import jax
import jax.numpy as jnp
from jax import lax
from jax.experimental import pallas as pl
from jax.experimental.pallas import tpu as pltpu
from jax.sharding import PartitionSpec as P

HEAD_DIM = 128
RATE_B = 4
LOG2E = 1.4426950408889634
NEG = -1e30
MESH = pl.DeviceIdType.MESH
F32 = jnp.float32
BF16 = jnp.bfloat16
NN = (((1,), (0,)), ((), ()))
NT = (((1,), (1,)), ((), ()))
TN = (((0,), (0,)), ((), ()))


def dot(a, b, dims=NN):
    return lax.dot_general(a, b, dims, preferred_element_type=F32)


def iota(shape, axis):
    return lax.broadcasted_iota(jnp.int32, shape, axis)


def one_hot(shape, condition):
    return jnp.where(condition, jnp.ones(shape, F32), jnp.zeros(shape, F32)).astype(BF16)


def late_residues(b, c):
    last = lax.rem(c, RATE_B)
    return jnp.where(last == b, lax.rem(b + 1, RATE_B), b), last


def place_of(r, second, last):
    free = r - jnp.where(second < r, 1, 0) - jnp.where(last < r, 1, 0)
    return jnp.where(last == r, 3, jnp.where(second == r, 2, free))


def stat_rows(count, level):
    high = level.astype(BF16).astype(F32)
    rest = level - high
    mid = rest.astype(BF16).astype(F32)
    low = rest - mid
    row = iota((count, level.shape[1]), 0)
    zero = jnp.zeros((count, level.shape[1]), F32)
    return jnp.where(row == 0, high, jnp.where(row == 1, mid, jnp.where(row == 2, low, zero)))


def kernel(
    q_hbm, k_hbm, v_hbm, offs_b, offs_c, w_hbm, out_hbm,
    qv, kv, vv, mkv, wv, qp, qf, kf, vf, nat, st1b, st1c, rc1b, rc1c, ckv, oa, la,
    rbst, rbrc, rcst, rcrc, xs, from_left0, from_left1, across0, across1, from_right0, from_right1, att, acc, outv,
    ost, orc, osm,
    ld_s, mate_ss, mate_rs, p1c_ss, p1c_rs, p1b_ss, p1b_rs, zg_ss, zg_rs,
    rb_ss, rb_rs, rc_ss, rc_rs, x_ss, x_rs, f_ss, of_ss, of_rs, os_s, out_s, hello, plane_in, all_in,
):
    rows, width = qv.shape
    heads = width // HEAD_DIM
    half = rows // 2
    sel_b = rows // RATE_B
    sel_c = st1c.shape[1]
    top_stride = rows // sel_c
    scale = HEAD_DIM**-0.5 * LOG2E

    s = lax.axis_index("seq")
    y = lax.axis_index("head")
    ny = lax.axis_size("head")
    nz = lax.axis_size("seq") // heads
    z = s // heads
    i = s % heads
    core = s % 2
    right = (y + 1) % ny
    left = (y + ny - 1) % ny

    def plane(j):
        return {"seq": z * heads + j}

    def along_z(t):
        return {"seq": t * heads + i}

    def remote(src, dst, ssem, rsem, device):
        return pltpu.make_async_remote_copy(
            src_ref=src, dst_ref=dst, send_sem=ssem, recv_sem=rsem, device_id=device, device_id_type=MESH
        )

    chunk = 256
    loads = [
        pltpu.make_async_copy(src, dst, ld_s.at[n])
        for n, (src, dst) in enumerate(((q_hbm, qv), (k_hbm, kv), (v_hbm, vv), (w_hbm, wv)))
    ]
    for copy in loads[:3]:
        copy.start()

    barrier = pltpu.get_barrier_semaphore()
    greeter = i == 2 * y
    peers = (heads - 1) + (ny - 1)
    ckv[...] = jnp.zeros(ckv.shape, BF16)

    def greet_plane(d, _):
        j = (i + d) % heads

        @pl.when(jnp.logical_or(greeter, j != 2 * y))
        def _():
            pl.semaphore_signal(barrier, 1, device_id=plane(j), device_id_type=MESH)

        return 0

    def each_plane(condition, act):
        def step(t, _):
            pl.when(condition(t))(lambda: act(t))
            return 0

        lax.fori_loop(0, nz, step, 0)

    def each_group(act):
        for d in range(1, 4):
            act((y + d) % ny)

    def greet_group(other):
        @pl.when(jnp.logical_or(greeter, i != 2 * other))
        def _():
            pl.semaphore_signal(barrier, 1, device_id={"head": other}, device_id_type=MESH)

    each_group(greet_group)
    lax.fori_loop(1, heads, greet_plane, 0)

    @pl.when(greeter)
    def _():
        def up(t):
            pl.semaphore_signal(barrier, 1, device_id=along_z(t), device_id_type=MESH)

        each_plane(lambda t: t > z, up)

    table = jnp.zeros((heads, 128), jnp.int32)
    for h in range(heads):
        second, last = late_residues(offs_b[z, h], offs_c[0, h])
        pair = jnp.where(iota((heads, 128), 1) == 0, second, last)
        table = jnp.where(iota((heads, 128), 0) == h, pair, table)
    ost[...] = table
    own_table = pltpu.make_async_copy(ost, osm.at[0], os_s.at[0])
    own_table.start()

    for copy, field, wide in zip(loads, (qv, kv, vv), (qf, kf, vf)):
        copy.wait()
        for h in range(heads):
            wide[h] = field[:, h * HEAD_DIM : (h + 1) * HEAD_DIM].astype(F32)

    def pick(j, _):
        b = offs_b[z, j]
        c = offs_c[0, j]
        cols = pl.ds(pl.multiple_of(j * HEAD_DIM, HEAD_DIM), HEAD_DIM)
        for n, wide in enumerate((qf, kf, vf)):
            part = slice(n * HEAD_DIM, (n + 1) * HEAD_DIM)
            st1c[j, :, part] = wide[j, pl.ds(c, sel_c, stride=top_stride), :].astype(BF16)
            st1b[j, :, part] = wide[j, pl.ds(b, sel_b, stride=RATE_B), :].astype(BF16)
        for r in range(RATE_B):
            qp[r * sel_b : (r + 1) * sel_b, cols] = qf[j, pl.ds(r, sel_b, stride=RATE_B), :].astype(BF16)
        return 0

    lax.fori_loop(0, heads, pick, 0)

    @pl.when(jnp.logical_not(greeter))
    def _():
        pl.semaphore_wait(barrier, peers)
        pl.semaphore_signal(hello, 1, device_id=plane(2 * y), device_id_type=MESH)

        def say(other):
            @pl.when(i == 2 * other)
            def _():
                pl.semaphore_signal(hello, 1, device_id={"head": other}, device_id_type=MESH)

        each_group(say)

    @pl.when(greeter)
    def _():
        pl.semaphore_wait(hello, peers)

    def mate_copy(n, device):
        cols = pl.ds((n // 2) * chunk, chunk)
        src, dst = (kv, vv)[n % 2], mkv.at[n % 2]
        return remote(src.at[:, cols], dst.at[:, cols], mate_ss.at[n], mate_rs.at[n], device)

    mates = 2 * (width // chunk)

    def mate_start(first, last):
        @pl.when(core == 0)
        def _():
            for n in range(first, last):
                mate_copy(n, plane(i + 1)).start()

    mate_start(0, 2)

    def table_copy(d):
        return remote(ost, orc.at[d - 1], of_ss.at[d - 1], of_rs.at[d - 1], {"head": (y + d) % ny})

    def p1c(j, src):
        return remote(st1c.at[j], rc1c.at[src], p1c_ss.at[j], p1c_rs.at[src], plane(j))

    def p1b(j, src):
        return remote(st1b.at[j], rc1b.at[src], p1b_ss.at[j], p1b_rs.at[src], plane(j))

    def send_c(d, _):
        p1c((i + d) % heads, i).start()
        return 0

    def send_b(d, _):
        p1b((i + d) % heads, i).start()
        return 0

    lax.fori_loop(1, heads, send_c, 0)
    lax.fori_loop(1, heads, send_b, 0)
    mate_start(2, mates)
    for d in range(1, 4):
        table_copy(d).start()
    loads[3].start()
    rc1b[i] = st1b[i]
    rc1c[i] = st1c[i]

    landing = ((from_left0, from_left1), (across0, across1), (from_right0, from_right1))
    few = heads // 2

    def blocks(ref, h, part):
        return ref.at[h, pl.ds(0, 2)] if part == 0 else ref.at[h, pl.ds(part + 1, 1)]

    def x_copy(h, part, to_right, group):
        n, slot = (0, 0) if to_right else (1, 2)
        device = {"head": right if to_right else left}
        dst = blocks(landing[slot][group], h % few, part)
        return remote(blocks(xs, h, part), dst, x_ss.at[n, h, part], x_rs.at[slot, h, part], device)

    def x_send(h, part):
        for group in range(2):

            @pl.when(h // few == group)
            def _():
                x_copy(h, part, True, group).start()
                x_copy(h, part, False, group).start()

    def x_recv(slot, h, part, group):
        dst = blocks(landing[slot][group], h % few, part)
        return remote(blocks(xs, h, part), dst, f_ss.at[h, part], x_rs.at[slot, h, part], {"head": right})

    def x_forward(h, part, to_right, group):
        device = {"head": right if to_right else left}
        src = blocks(landing[0 if to_right else 2][group], h % few, part)
        dst = blocks(landing[1][group], h % few, part)
        return remote(src, dst, f_ss.at[h, part], x_rs.at[1, h, part], device)

    def forward(part, group):
        def step(n, _):
            h = group * few + n
            x_recv(0, h, part, group).wait_recv()
            x_recv(2, h, part, group).wait_recv()

            @pl.when(h % 2 == 0)
            def _():
                x_forward(h, part, True, group).start()

            @pl.when(h % 2 == 1)
            def _():
                x_forward(h, part, False, group).start()

            return 0

        lax.fori_loop(0, few, step, 0)

    def attend(key_parts, value_parts, query):
        scores = []
        for keys, allowed in key_parts:
            part = dot(keys, query, NT) * scale
            scores.append(part if allowed is None else jnp.where(allowed, part, NEG))
        top = functools.reduce(jnp.maximum, [jnp.max(part, axis=0, keepdims=True) for part in scores])
        weights = [jnp.exp2(part - top) for part in scores]
        total = functools.reduce(jnp.add, [jnp.sum(part, axis=0, keepdims=True) for part in weights])
        numer = functools.reduce(
            jnp.add, [dot(values, part.astype(BF16), TN) for values, part in zip(value_parts, weights)]
        )
        return numer / total, top + jnp.log2(total)

    def lowest(h, with_mate):
        cols = pl.ds(pl.multiple_of(h * HEAD_DIM, HEAD_DIM), HEAD_DIM)
        for n in range(2):
            column = iota((rows, half), 1)
            residue = jnp.where(column < sel_b, 2 * n, 2 * n + 1 - RATE_B * sel_b)
            causal = iota((rows, half), 0) <= RATE_B * column + residue
            key_parts = [(kv[:, cols], causal)]
            value_parts = [vv[:, cols]]
            if with_mate:
                key_parts.append((mkv[0, :, cols], None))
                value_parts.append(mkv[1, :, cols])
            out, level = attend(key_parts, value_parts, qp[n * half : (n + 1) * half, cols])
            for t in range(2):
                part = slice(t * sel_b, (t + 1) * sel_b)
                oa[h, 2 * n + t] = out[:, part]
                la[h, 2 * n + t] = jnp.broadcast_to(level[:, part], (8, sel_b))

    def zg(t, src):
        return remote(ckv.at[src], ckv.at[src], zg_ss.at[t], zg_rs.at[src], along_z(t))

    def lowest_level(h, _):
        @pl.when(core == 1)
        def _():
            for n in range(mates // 2):

                @pl.when(h == n * (chunk // HEAD_DIM))
                def _():
                    for m in range(2):
                        mate_copy(2 * n + m, plane(i - 1)).wait_recv()

            lowest(h, True)

        @pl.when(core == 0)
        def _():
            lowest(h, False)

        second, last = late_residues(offs_b[z, h], offs_c[0, h])
        zero_free = jnp.logical_and(second != 0, last != 0)
        one_free = jnp.logical_and(second != 1, last != 1)
        three_free = jnp.logical_and(second != 3, last != 3)
        two_free = jnp.logical_and(second != 2, last != 2)
        xs[h, 0] = oa[h, jnp.where(zero_free, 0, jnp.where(one_free, 1, 2))].T.astype(BF16)
        xs[h, 1] = oa[h, jnp.where(three_free, 3, jnp.where(two_free, 2, 1))].T.astype(BF16)
        x_send(h, 0)

        @pl.when(jnp.logical_and(h == 0, jnp.logical_and(greeter, z > 0)))
        def _():
            pl.semaphore_wait(barrier, z)

            def down(t):
                pl.semaphore_signal(plane_in, 1, device_id=along_z(t), device_id_type=MESH)

            each_plane(lambda t: t < z, down)

        @pl.when(jnp.logical_and(h == 4, greeter))
        def _():
            @pl.when(z < nz - 1)
            def _():
                pl.semaphore_wait(plane_in, nz - 1 - z)

            def tell(d, _):
                pl.semaphore_signal(all_in, 1, device_id=plane((i + d) % heads), device_id_type=MESH)
                return 0

            lax.fori_loop(1, heads, tell, 0)

        @pl.when(h == 5)
        def _():
            def wait_c(d, _):
                p1c(i, (i + d) % heads).wait_recv()
                return 0

            lax.fori_loop(1, heads, wait_c, 0)
            for j in range(heads):
                ckv[z, j * sel_c : (j + 1) * sel_c, :] = rc1c[j, :, HEAD_DIM:]

            @pl.when(jnp.logical_not(greeter))
            def _():
                pl.semaphore_wait(all_in, 1)

            each_plane(lambda t: t > z, lambda t: zg(t, z).start())

        return 0

    lax.fori_loop(0, heads, lowest_level, 0)

    forward(0, 0)

    def wait_b(d, _):
        p1b(i, (i + d) % heads).wait_recv()
        return 0

    lax.fori_loop(1, heads, wait_b, 0)

    def rb(j, src):
        return remote(rbst.at[j], rbrc.at[src], rb_ss.at[j], rb_rs.at[src], plane(j))

    def rc(j, src):
        return remote(rcst.at[j], rcrc.at[src], rc_ss.at[j], rc_rs.at[src], plane(j))

    def field_b(first, last, n):
        part = rc1b[first:last, :, n * HEAD_DIM : (n + 1) * HEAD_DIM]
        return part.reshape((last - first) * sel_b, HEAD_DIM)

    for pair in range(heads // 2):
        first = 2 * pair
        block = 2 * sel_b
        causal = iota((block, block), 0) <= iota((block, block), 1)
        key_parts = [(field_b(first, first + 2, 1), causal)]
        value_parts = [field_b(first, first + 2, 2)]
        if pair:
            key_parts.append((field_b(0, first, 1), None))
            value_parts.append(field_b(0, first, 2))
        out, level = attend(key_parts, value_parts, field_b(first, first + 2, 0))
        stats = stat_rows(16, level)
        for n in range(2):
            cols = slice(n * sel_b, (n + 1) * sel_b)
            rbst[first + n, :HEAD_DIM] = out[:, cols].astype(BF16)
            rbst[first + n, HEAD_DIM:] = stats[:, cols].astype(BF16)

            @pl.when(first + n != i)
            def _():
                rb(first + n, i).start()

    rbrc[i] = rbst[i]

    forward(0, 1)

    def level_of(field):
        return jnp.sum(field[HEAD_DIM : HEAD_DIM + 8].astype(F32), axis=0, keepdims=True)

    def merge(h, residue, others):
        level_a = la[h, residue][0:1]
        peak = functools.reduce(jnp.maximum, [level for _, level in others], level_a)
        factor = jnp.exp2(level_a - peak)
        numer = factor * oa[h, residue]
        denom = factor
        for field, level in others:
            factor = jnp.exp2(level - peak)
            numer = numer + factor * field
            denom = denom + factor
        return (numer / denom).T.astype(BF16)

    def merge_second(h, _):
        @pl.when(h != i)
        def _():
            rb(i, h).wait_recv()

        b = offs_b[z, h]
        second, _ = late_residues(b, offs_c[0, h])
        level_b = jnp.where(second == b, level_of(rbrc[h]), NEG)
        xs[h, 2] = merge(h, second, [(rbrc[h, :HEAD_DIM].astype(F32), level_b)])
        x_send(h, 1)
        return 0

    lax.fori_loop(0, heads, merge_second, 0)

    each_plane(lambda t: t < z, lambda t: zg(z, t).wait_recv())
    count_c = heads * sel_c
    keys_c = ckv[:, :, :HEAD_DIM].reshape(nz * count_c, HEAD_DIM)
    values_c = ckv[:, :, HEAD_DIM:].reshape(nz * count_c, HEAD_DIM)
    query_c = rc1c[:, :, :HEAD_DIM].reshape(count_c, HEAD_DIM)
    shape_c = (nz * count_c, count_c)
    allowed_c = iota(shape_c, 0) <= iota(shape_c, 1) + z * count_c
    out, level = attend([(keys_c, allowed_c)], [values_c], query_c)
    flat = jnp.concatenate([out.T, stat_rows(HEAD_DIM, level).T], axis=1).astype(BF16)
    rcst[...] = flat.reshape(heads, sel_c, 2 * HEAD_DIM)
    rcrc[i] = rcst[i]

    def send_rc(d, _):
        rc((i + d) % heads, i).start()
        return 0

    lax.fori_loop(1, heads, send_rc, 0)

    forward(1, 0)

    def merge_last(h, _):
        @pl.when(h != i)
        def _():
            rc(i, h).wait_recv()

        b = offs_b[z, h]
        c = offs_c[0, h]
        _, last = late_residues(b, c)
        spot = lax.div(c, RATE_B)
        apart = top_stride // RATE_B
        put = one_hot((sel_c, sel_b), iota((sel_c, sel_b), 1) == apart * iota((sel_c, sel_b), 0) + spot)
        from_c = dot(rcrc[h], put, TN)
        level_b = jnp.where(last == b, level_of(rbrc[h]), NEG)
        level_c = jnp.where(lax.rem(iota((1, sel_b), 1), apart) == spot, level_of(from_c), NEG)
        xs[h, 3] = merge(h, last, [(rbrc[h, :HEAD_DIM].astype(F32), level_b), (from_c[:HEAD_DIM], level_c)])
        x_send(h, 2)
        return 0

    lax.fori_loop(0, heads, merge_last, 0)
    forward(1, 1)

    own_table.wait()
    for d in range(1, 4):
        table_copy(d).wait_recv()
    tables = [pltpu.make_async_copy(orc.at[d - 1], osm.at[d], os_s.at[d]) for d in range(1, 4)]
    for copy in tables:
        copy.start()
    for copy in tables:
        copy.wait()
    loads[3].wait()

    def store(n):
        cols = pl.ds(pl.multiple_of(n * chunk, chunk), chunk)
        return pltpu.make_async_copy(outv.at[:, cols], out_hbm.at[:, cols], out_s.at[n])

    def project(d, ref, first, count, fresh, final=False):
        def place(n, _):
            h = first + n
            cols = pl.ds(pl.multiple_of(h * HEAD_DIM, HEAD_DIM), HEAD_DIM)
            for r in range(RATE_B):
                att[d, r * sel_b : (r + 1) * sel_b, cols] = ref[n, place_of(r, osm[d, h, 0], osm[d, h, 1])]
            return 0

        lax.fori_loop(0, count, place, 0)
        group = (y + ny - d) % ny
        depth = count * HEAD_DIM
        at = pl.multiple_of(group * width + first * HEAD_DIM, HEAD_DIM)

        def columns(n, _):
            cols = pl.ds(pl.multiple_of(n * chunk, chunk), chunk)
            part = dot(att[d, :, first * HEAD_DIM : first * HEAD_DIM + depth], wv[pl.ds(at, depth), cols])
            if fresh:
                acc[:, cols] = part
            elif final:
                total = acc[:, cols] + part
                for t in range(chunk // 128):
                    for r in range(RATE_B):
                        block = total[r * sel_b : (r + 1) * sel_b, t * 128 : (t + 1) * 128]
                        nat[n, t, pl.ds(r, sel_b, stride=RATE_B), :] = block
                outv[:, cols] = jnp.concatenate([nat[n, t] for t in range(chunk // 128)], axis=1).astype(BF16)
                store(n).start()
            else:
                acc[:, cols] += part
            return 0

        lax.fori_loop(0, width // chunk, columns, 0)

    project(0, xs, 0, heads, True)
    for group in range(2):
        forward(2, group)
        project(1, from_left0 if group == 0 else from_left1, group * few, few, False)
        project(3, from_right0 if group == 0 else from_right1, group * few, few, False)
    @pl.when(core == 0)
    def _():
        for n in range(mates):
            mate_copy(n, plane(i + 1)).wait_send()

    for d in range(1, 4):
        table_copy(d).wait_send()

    def sent_plane(d, _):
        j = (i + d) % heads
        p1c(j, i).wait_send()
        p1b(j, i).wait_send()
        rb(j, i).wait_send()
        rc(j, i).wait_send()
        return 0

    lax.fori_loop(1, heads, sent_plane, 0)

    each_plane(lambda t: t > z, lambda t: zg(t, z).wait_send())

    def sent_y(h, _):
        for part in range(3):
            x_copy(h, part, True, 0).wait_send()
            x_copy(h, part, False, 0).wait_send()
            x_forward(h, part, True, 0).wait_send()
        return 0

    for group in range(2):

        def arrived(n, _):
            for part in range(3):
                x_recv(1, group * few + n, part, group).wait_recv()
            return 0

        lax.fori_loop(0, few, arrived, 0)
        if group == 1:
            lax.fori_loop(0, heads, sent_y, 0)
        project(2, landing[1][group], group * few, few, False, group == 1)

    for n in range(width // chunk):
        store(n).wait()


def shards(queries, keys, values, offsets_b, offsets_c, out_weight):
    rows, width = queries.shape
    depth, features = out_weight.shape
    heads = width // HEAD_DIM
    nz = lax.axis_size("seq") // heads
    ny = lax.axis_size("head")
    sel_b = rows // RATE_B
    sel_c = rows // (lax.axis_size("seq") // 2)
    three = 3 * HEAD_DIM
    dma = pltpu.SemaphoreType.DMA
    hbm = pl.BlockSpec(memory_space=pl.ANY)
    smem = pl.BlockSpec(memory_space=pltpu.SMEM)
    scratch = [
        pltpu.VMEM((rows, width), BF16),
        pltpu.VMEM((rows, width), BF16),
        pltpu.VMEM((rows, width), BF16),
        pltpu.VMEM((2, rows, width), BF16),
        pltpu.VMEM((depth, features), BF16),
        pltpu.VMEM((rows, width), BF16),
        *[pltpu.VMEM((heads, rows, HEAD_DIM), F32) for _ in range(3)],
        pltpu.VMEM((features // 256, 2, rows, 128), F32),
        pltpu.VMEM((heads, sel_b, three), BF16),
        pltpu.VMEM((heads, sel_c, three), BF16),
        pltpu.VMEM((heads, sel_b, three), BF16),
        pltpu.VMEM((heads, sel_c, three), BF16),
        pltpu.VMEM((nz, heads * sel_c, 2 * HEAD_DIM), BF16),
        pltpu.VMEM((heads, RATE_B, HEAD_DIM, sel_b), F32),
        pltpu.VMEM((heads, RATE_B, 8, sel_b), F32),
        pltpu.VMEM((heads, HEAD_DIM + 16, sel_b), BF16),
        pltpu.VMEM((heads, HEAD_DIM + 16, sel_b), BF16),
        pltpu.VMEM((heads, sel_c, 2 * HEAD_DIM), BF16),
        pltpu.VMEM((heads, sel_c, 2 * HEAD_DIM), BF16),
        pltpu.VMEM((heads, RATE_B, sel_b, HEAD_DIM), BF16),
        *[pltpu.VMEM((heads // 2, RATE_B, sel_b, HEAD_DIM), BF16) for _ in range(6)],
        pltpu.VMEM((ny, rows, width), BF16),
        pltpu.VMEM((rows, features), F32),
        pltpu.VMEM((rows, features), BF16),
        pltpu.VMEM((heads, 128), jnp.int32),
        pltpu.VMEM((3, heads, 128), jnp.int32),
        pltpu.SMEM((ny, heads, 128), jnp.int32),
        dma((4,)),
        dma((2 * (width // 256),)),
        dma((2 * (width // 256),)),
        dma((heads,)),
        dma((heads,)),
        dma((heads,)),
        dma((heads,)),
        dma((nz,)),
        dma((nz,)),
        dma((heads,)),
        dma((heads,)),
        dma((heads,)),
        dma((heads,)),
        dma((2, heads, 3)),
        dma((3, heads, 3)),
        dma((heads, 3)),
        dma((3,)),
        dma((3,)),
        dma((ny,)),
        dma((features // 256,)),
        *[pltpu.SemaphoreType.REGULAR for _ in range(3)],
    ]
    return pl.pallas_call(
        kernel,
        out_shape=jax.ShapeDtypeStruct((rows, features), BF16),
        in_specs=[hbm, hbm, hbm, smem, smem, hbm],
        out_specs=hbm,
        scratch_shapes=scratch,
        compiler_params=pltpu.CompilerParams(
            collective_id=0, has_side_effects=True, vmem_limit_bytes=56 * 2**20
        ),
    )(queries, keys, values, offsets_b, offsets_c.reshape(1, heads), out_weight)


def solution(mesh):
    placed = (
        P("seq", "head"),
        P("seq", "head"),
        P("seq", "head"),
        P(None, "head"),
        P("head"),
        P(None, "head"),
    )
    return jax.shard_map(
        shards, mesh=mesh, in_specs=placed, out_specs=P("seq", "head"), check_vma=False
    )
```

time: 63 us -> 55.8 us (0.89)
  the two profiles are of different devices: /device:TPU:36 before, /device:TPU:1 now
where the time goes in v2:
time: 55.8 us; the launch traced here: 55.7 us
  Pallas kernels  53.4 us (96%)
  local copies, waits for them, and re-layouts  2.26 us (4%)
    pallas_call x1, Pallas kernels, shards(): pl.pallas_call(kernel, out_shape=jax.ShapeDtypeStruct((rows, features), B...  53.4 us
    unnamed x1, local copies, waits for them, and re-layouts  2.26 us

profile of v2, /device:TPU:1, one launch (start us, length us, event | category | flops | bytes accessed | tf_op | source)
XLA Modules:
  0.0 55.7 jit_solution(10345977949046082781)
XLA Ops:
  0.0 53.4 %shard_map.64 = bf16[512,1024]{1,0:T(8,128)(2,1)} custom-call(bf16[512,1024]{1,0:T(8,128)(2,1)} %q_hbm.1, bf16[512,1024]{1,0:T(8,128)(2,1)} %k_hbm.1, bf16[512,1024]{1,0:T(8,128)(2,1)} %v_hbm.1, s32[8,8]{1,0:T(8,128)} %offs_b.1, s32[1,8]{1,0:T(1,128)} %bitcast.1, bf16[4096,1024]{1,0:T(8,128)(2,1)} %w_hbm.1), custom_call_target="tpu_custom_call" | custom-call | tf_op jit(solution)/shard_map/pallas_call | solution.py:639
  53.4 2.3 %copy.8 = bf16[512,1024]{1,0:T(8,128)(2,1)} copy(bf16[512,1024]{1,0:T(8,128)(2,1)} %shard_map.64) | data formatting | bytes 2097152

commit v3 on v2

--- a/solution.py
+++ b/solution.py
@@ -52,12 +52,12 @@
 
 
 def kernel(
-    q_hbm, k_hbm, v_hbm, offs_b, offs_c, w_hbm, out_hbm,
+    q_hbm, k_hbm, v_hbm, offs_b, offs_c, w_hbm, out,
     qv, kv, vv, mkv, wv, qp, qf, kf, vf, nat, st1b, st1c, rc1b, rc1c, ckv, oa, la,
-    rbst, rbrc, rcst, rcrc, xs, from_left0, from_left1, across0, across1, from_right0, from_right1, att, acc, outv,
+    rbst, rbrc, rcst, rcrc, xs, from_left0, from_left1, across0, across1, from_right0, from_right1, att, acc,
     ost, orc, osm,
     ld_s, mate_ss, mate_rs, p1c_ss, p1c_rs, p1b_ss, p1b_rs, zg_ss, zg_rs,
-    rb_ss, rb_rs, rc_ss, rc_rs, x_ss, x_rs, f_ss, of_ss, of_rs, os_s, out_s, hello, plane_in, all_in,
+    rb_ss, rb_rs, rc_ss, rc_rs, x_ss, x_rs, f_ss, of_ss, of_rs, os_s, hello, plane_in, all_in,
 ):
     rows, width = qv.shape
     heads = width // HEAD_DIM
@@ -224,50 +224,62 @@
     landing = ((from_left0, from_left1), (across0, across1), (from_right0, from_right1))
     few = heads // 2
 
-    def blocks(ref, h, part):
-        return ref.at[h, pl.ds(0, 2)] if part == 0 else ref.at[h, pl.ds(part + 1, 1)]
-
-    def x_copy(h, part, to_right, group):
+    def units(part):
+        return heads if part == 0 else few
+
+    def blocks(ref, u, part):
+        return ref.at[u, pl.ds(0, 2)] if part == 0 else ref.at[pl.ds(2 * u, 2), pl.ds(part + 1, 1)]
+
+    def landed(slot, u, part, group):
+        return blocks(landing[slot][group], u % (units(part) // 2), part)
+
+    def x_copy(u, part, to_right, group):
         n, slot = (0, 0) if to_right else (1, 2)
         device = {"head": right if to_right else left}
-        dst = blocks(landing[slot][group], h % few, part)
-        return remote(blocks(xs, h, part), dst, x_ss.at[n, h, part], x_rs.at[slot, h, part], device)
-
-    def x_send(h, part):
+        dst = landed(slot, u, part, group)
+        return remote(blocks(xs, u, part), dst, x_ss.at[n, u, part], x_rs.at[slot, u, part], device)
+
+    def x_send(u, part):
         for group in range(2):
 
-            @pl.when(h // few == group)
+            @pl.when(u // (units(part) // 2) == group)
             def _():
-                x_copy(h, part, True, group).start()
-                x_copy(h, part, False, group).start()
-
-    def x_recv(slot, h, part, group):
-        dst = blocks(landing[slot][group], h % few, part)
-        return remote(blocks(xs, h, part), dst, f_ss.at[h, part], x_rs.at[slot, h, part], {"head": right})
-
-    def x_forward(h, part, to_right, group):
+                x_copy(u, part, True, group).start()
+                x_copy(u, part, False, group).start()
+
+    def x_recv(slot, u, part, group):
+        dst = landed(slot, u, part, group)
+        return remote(blocks(xs, u, part), dst, f_ss.at[u, part], x_rs.at[slot, u, part], {"head": right})
+
+    def x_forward(u, part, to_right, group):
         device = {"head": right if to_right else left}
-        src = blocks(landing[0 if to_right else 2][group], h % few, part)
-        dst = blocks(landing[1][group], h % few, part)
-        return remote(src, dst, f_ss.at[h, part], x_rs.at[1, h, part], device)
+        src = landed(0 if to_right else 2, u, part, group)
+        dst = landed(1, u, part, group)
+        return remote(src, dst, f_ss.at[u, part], x_rs.at[1, u, part], device)
+
+    def each_unit(part, group, act):
+        count = units(part) // 2
+
+        def step(n, _):
+            act(group * count + n)
+            return 0
+
+        lax.fori_loop(0, count, step, 0)
 
     def forward(part, group):
-        def step(n, _):
-            h = group * few + n
-            x_recv(0, h, part, group).wait_recv()
-            x_recv(2, h, part, group).wait_recv()
-
-            @pl.when(h % 2 == 0)
+        def act(u):
+            x_recv(0, u, part, group).wait_recv()
+            x_recv(2, u, part, group).wait_recv()
+
+            @pl.when(u % 2 == 0)
             def _():
-                x_forward(h, part, True, group).start()
-
-            @pl.when(h % 2 == 1)
+                x_forward(u, part, True, group).start()
+
+            @pl.when(u % 2 == 1)
             def _():
-                x_forward(h, part, False, group).start()
-
-            return 0
-
-        lax.fori_loop(0, few, step, 0)
+                x_forward(u, part, False, group).start()
+
+        each_unit(part, group, act)
 
     def attend(key_parts, value_parts, query):
         scores = []
@@ -280,7 +292,7 @@
         numer = functools.reduce(
             jnp.add, [dot(values, part.astype(BF16), TN) for values, part in zip(value_parts, weights)]
         )
-        return numer / total, top + jnp.log2(total)
+        return numer * (1.0 / total), top + jnp.log2(total)
 
     def lowest(h, with_mate):
         cols = pl.ds(pl.multiple_of(h * HEAD_DIM, HEAD_DIM), HEAD_DIM)
@@ -293,14 +305,16 @@
             if with_mate:
                 key_parts.append((mkv[0, :, cols], None))
                 value_parts.append(mkv[1, :, cols])
-            out, level = attend(key_parts, value_parts, qp[n * half : (n + 1) * half, cols])
+            result, level = attend(key_parts, value_parts, qp[n * half : (n + 1) * half, cols])
             for t in range(2):
                 part = slice(t * sel_b, (t + 1) * sel_b)
-                oa[h, 2 * n + t] = out[:, part]
+                oa[h, 2 * n + t] = result[:, part]
                 la[h, 2 * n + t] = jnp.broadcast_to(level[:, part], (8, sel_b))
 
     def zg(t, src):
         return remote(ckv.at[src], ckv.at[src], zg_ss.at[t], zg_rs.at[src], along_z(t))
+
+    go_up = jnp.where(z < 2, 6, 5)
 
     def lowest_level(h, _):
         @pl.when(core == 1)
@@ -336,7 +350,7 @@
 
             each_plane(lambda t: t < z, down)
 
-        @pl.when(jnp.logical_and(h == 4, greeter))
+        @pl.when(jnp.logical_and(h == go_up - 1, greeter))
         def _():
             @pl.when(z < nz - 1)
             def _():
@@ -348,7 +362,7 @@
 
             lax.fori_loop(1, heads, tell, 0)
 
-        @pl.when(h == 5)
+        @pl.when(h == go_up)
         def _():
             def wait_c(d, _):
                 p1c(i, (i + d) % heads).wait_recv()
@@ -367,6 +381,7 @@
         return 0
 
     lax.fori_loop(0, heads, lowest_level, 0)
+
 
     forward(0, 0)
 
@@ -395,11 +410,11 @@
         if pair:
             key_parts.append((field_b(0, first, 1), None))
             value_parts.append(field_b(0, first, 2))
-        out, level = attend(key_parts, value_parts, field_b(first, first + 2, 0))
+        result, level = attend(key_parts, value_parts, field_b(first, first + 2, 0))
         stats = stat_rows(16, level)
         for n in range(2):
             cols = slice(n * sel_b, (n + 1) * sel_b)
-            rbst[first + n, :HEAD_DIM] = out[:, cols].astype(BF16)
+            rbst[first + n, :HEAD_DIM] = result[:, cols].astype(BF16)
             rbst[first + n, HEAD_DIM:] = stats[:, cols].astype(BF16)
 
             @pl.when(first + n != i)
@@ -407,8 +422,8 @@
                 rb(first + n, i).start()
 
     rbrc[i] = rbst[i]
-
     forward(0, 1)
+
 
     def level_of(field):
         return jnp.sum(field[HEAD_DIM : HEAD_DIM + 8].astype(F32), axis=0, keepdims=True)
@@ -416,14 +431,12 @@
     def merge(h, residue, others):
         level_a = la[h, residue][0:1]
         peak = functools.reduce(jnp.maximum, [level for _, level in others], level_a)
-        factor = jnp.exp2(level_a - peak)
-        numer = factor * oa[h, residue]
-        denom = factor
-        for field, level in others:
-            factor = jnp.exp2(level - peak)
-            numer = numer + factor * field
-            denom = denom + factor
-        return (numer / denom).T.astype(BF16)
+        factors = [jnp.exp2(level - peak) for level in [level_a] + [level for _, level in others]]
+        share = 1.0 / functools.reduce(jnp.add, factors)
+        numer = (factors[0] * share) * oa[h, residue]
+        for (field, _), factor in zip(others, factors[1:]):
+            numer = numer + (factor * share) * field
+        return numer.T.astype(BF16)
 
     def merge_second(h, _):
         @pl.when(h != i)
@@ -434,7 +447,11 @@
         second, _ = late_residues(b, offs_c[0, h])
         level_b = jnp.where(second == b, level_of(rbrc[h]), NEG)
         xs[h, 2] = merge(h, second, [(rbrc[h, :HEAD_DIM].astype(F32), level_b)])
-        x_send(h, 1)
+
+        @pl.when(h % 2 == 1)
+        def _():
+            x_send(h // 2, 1)
+
         return 0
 
     lax.fori_loop(0, heads, merge_second, 0)
@@ -446,8 +463,8 @@
     query_c = rc1c[:, :, :HEAD_DIM].reshape(count_c, HEAD_DIM)
     shape_c = (nz * count_c, count_c)
     allowed_c = iota(shape_c, 0) <= iota(shape_c, 1) + z * count_c
-    out, level = attend([(keys_c, allowed_c)], [values_c], query_c)
-    flat = jnp.concatenate([out.T, stat_rows(HEAD_DIM, level).T], axis=1).astype(BF16)
+    result, level = attend([(keys_c, allowed_c)], [values_c], query_c)
+    flat = jnp.concatenate([result.T, stat_rows(HEAD_DIM, level).T], axis=1).astype(BF16)
     rcst[...] = flat.reshape(heads, sel_c, 2 * HEAD_DIM)
     rcrc[i] = rcst[i]
 
@@ -457,7 +474,6 @@
 
     lax.fori_loop(1, heads, send_rc, 0)
 
-    forward(1, 0)
 
     def merge_last(h, _):
         @pl.when(h != i)
@@ -474,10 +490,15 @@
         level_b = jnp.where(last == b, level_of(rbrc[h]), NEG)
         level_c = jnp.where(lax.rem(iota((1, sel_b), 1), apart) == spot, level_of(from_c), NEG)
         xs[h, 3] = merge(h, last, [(rbrc[h, :HEAD_DIM].astype(F32), level_b), (from_c[:HEAD_DIM], level_c)])
-        x_send(h, 2)
+
+        @pl.when(h % 2 == 1)
+        def _():
+            x_send(h // 2, 2)
+
         return 0
 
     lax.fori_loop(0, heads, merge_last, 0)
+    forward(1, 0)
     forward(1, 1)
 
     own_table.wait()
@@ -489,10 +510,6 @@
     for copy in tables:
         copy.wait()
     loads[3].wait()
-
-    def store(n):
-        cols = pl.ds(pl.multiple_of(n * chunk, chunk), chunk)
-        return pltpu.make_async_copy(outv.at[:, cols], out_hbm.at[:, cols], out_s.at[n])
 
     def project(d, ref, first, count, fresh, final=False):
         def place(n, _):
@@ -518,8 +535,7 @@
                     for r in range(RATE_B):
                         block = total[r * sel_b : (r + 1) * sel_b, t * 128 : (t + 1) * 128]
                         nat[n, t, pl.ds(r, sel_b, stride=RATE_B), :] = block
-                outv[:, cols] = jnp.concatenate([nat[n, t] for t in range(chunk // 128)], axis=1).astype(BF16)
-                store(n).start()
+                out[:, cols] = jnp.concatenate([nat[n, t] for t in range(chunk // 128)], axis=1).astype(BF16)
             else:
                 acc[:, cols] += part
             return 0
@@ -551,27 +567,19 @@
 
     each_plane(lambda t: t > z, lambda t: zg(t, z).wait_send())
 
-    def sent_y(h, _):
+    def sent_y(u, part):
+        x_copy(u, part, True, 0).wait_send()
+        x_copy(u, part, False, 0).wait_send()
+        x_forward(u, part, True, 0).wait_send()
+
+    for group in range(2):
+        if group == 1:
+            for part in range(3):
+                for half_of in range(2):
+                    each_unit(part, half_of, lambda u, part=part: sent_y(u, part))
         for part in range(3):
-            x_copy(h, part, True, 0).wait_send()
-            x_copy(h, part, False, 0).wait_send()
-            x_forward(h, part, True, 0).wait_send()
-        return 0
-
-    for group in range(2):
-
-        def arrived(n, _):
-            for part in range(3):
-                x_recv(1, group * few + n, part, group).wait_recv()
-            return 0
-
-        lax.fori_loop(0, few, arrived, 0)
-        if group == 1:
-            lax.fori_loop(0, heads, sent_y, 0)
+            each_unit(part, group, lambda u, part=part: x_recv(1, u, part, group).wait_recv())
         project(2, landing[1][group], group * few, few, False, group == 1)
-
-    for n in range(width // chunk):
-        store(n).wait()
 
 
 def shards(queries, keys, values, offsets_b, offsets_c, out_weight):
@@ -610,7 +618,6 @@
         *[pltpu.VMEM((heads // 2, RATE_B, sel_b, HEAD_DIM), BF16) for _ in range(6)],
         pltpu.VMEM((ny, rows, width), BF16),
         pltpu.VMEM((rows, features), F32),
-        pltpu.VMEM((rows, features), BF16),
         pltpu.VMEM((heads, 128), jnp.int32),
         pltpu.VMEM((3, heads, 128), jnp.int32),
         pltpu.SMEM((ny, heads, 128), jnp.int32),
@@ -633,17 +640,16 @@
         dma((3,)),
         dma((3,)),
         dma((ny,)),
-        dma((features // 256,)),
         *[pltpu.SemaphoreType.REGULAR for _ in range(3)],
     ]
     return pl.pallas_call(
         kernel,
         out_shape=jax.ShapeDtypeStruct((rows, features), BF16),
         in_specs=[hbm, hbm, hbm, smem, smem, hbm],
-        out_specs=hbm,
+        out_specs=pl.BlockSpec(memory_space=pltpu.VMEM),
         scratch_shapes=scratch,
         compiler_params=pltpu.CompilerParams(
-            collective_id=0, has_side_effects=True, vmem_limit_bytes=56 * 2**20
+            collective_id=0, has_side_effects=True, vmem_limit_bytes=52 * 2**20
         ),
     )(queries, keys, values, offsets_b, offsets_c.reshape(1, heads), out_weight)
 

time: 55.8 us -> 53.5 us (0.959)
  Pallas kernels: 53.4 us -> 51 us
    pallas_call x1, Pallas kernels: 53.4 us -> 51 us  [shards(): pl.pallas_call(kernel, out_shape=jax.ShapeDtypeStruct((rows, features), B...]
    unnamed x1 -> x5, local copies, waits for them, and re-layouts: 2.26 us -> 2.31 us
where the time goes in v3:
time: 53.5 us; the launch traced here: 53.3 us
  Pallas kernels  51 us (95%)
  local copies, waits for them, and re-layouts  2.31 us (4%)
    pallas_call x1, Pallas kernels, shards(): pl.pallas_call(kernel, out_shape=jax.ShapeDtypeStruct((rows, features), B...  51 us
    unnamed x5, local copies, waits for them, and re-layouts  2.31 us

profile of v3, /device:TPU:1, one launch (start us, length us, event | category | flops | bytes accessed | tf_op | source)
XLA Modules:
  0.0 53.3 jit_solution(13707871927714382177)
XLA Ops:
  0.0 0.0 copy-start
  0.0 0.7 %copy-done = s32[8,8]{1,0:T(8,128)S(1)} copy-done((s32[8,8]{1,0:T(8,128)S(1)}, s32[8,8]{1,0:T(8,128)}, u32[]{:S(2)}) %copy-start) | copy-done | bytes 280
  0.7 0.0 copy-start.1
  0.7 0.7 %copy-done.1 = s32[8]{0:T(128)S(1)} copy-done((s32[8]{0:T(128)S(1)}, s32[8]{0:T(128)}, u32[]{:S(2)}) %copy-start.1) | copy-done | bytes 56
  1.3 51.0 %shard_map.64 = bf16[512,1024]{1,0:T(8,128)(2,1)S(1)} custom-call(bf16[512,1024]{1,0:T(8,128)(2,1)} %q_hbm.1, bf16[512,1024]{1,0:T(8,128)(2,1)} %k_hbm.1, bf16[512,1024]{1,0:T(8,128)(2,1)} %v_hbm.1, s32[8,8]{1,0:T(8,128)S(1)} %copy-done, s32[1,8]{1,0:T(1,128)S(1)} %bitcast.1, bf16[4096,1024]{1,0:T(8,128)(2,1)} %w_hbm.1), custom_call_target="tpu_custom_call" | custom-call | tf_op jit(solution)/shard_map/pallas_call | solution.py:645
  52.4 1.0 %copy.8 = bf16[512,1024]{1,0:T(8,128)(2,1)} copy(bf16[512,1024]{1,0:T(8,128)(2,1)S(1)} %shard_map.64) | data formatting | bytes 2097152
Async XLA Ops:
  0.0 0.7 %copy-start = (s32[8,8]{1,0:T(8,128)S(1)}, s32[8,8]{1,0:T(8,128)}, u32[]{:S(2)}) copy-start(s32[8,8]{1,0:T(8,128)} %offs_b.1) | copy-start | bytes 772
  0.7 0.7 %copy-start.1 = (s32[8]{0:T(128)S(1)}, s32[8]{0:T(128)}, u32[]{:S(2)}) copy-start(s32[8]{0:T(128)} %param.10) | copy-start | bytes 100

commit v4 on v3

--- a/solution.py
+++ b/solution.py
@@ -148,7 +148,7 @@
     for copy, field, wide in zip(loads, (qv, kv, vv), (qf, kf, vf)):
         copy.wait()
         for h in range(heads):
-            wide[h] = field[:, h * HEAD_DIM : (h + 1) * HEAD_DIM].astype(F32)
+            wide[h, :rows] = field[:, h * HEAD_DIM : (h + 1) * HEAD_DIM].astype(F32)
 
     def pick(j, _):
         b = offs_b[z, j]
@@ -535,7 +535,7 @@
                     for r in range(RATE_B):
                         block = total[r * sel_b : (r + 1) * sel_b, t * 128 : (t + 1) * 128]
                         nat[n, t, pl.ds(r, sel_b, stride=RATE_B), :] = block
-                out[:, cols] = jnp.concatenate([nat[n, t] for t in range(chunk // 128)], axis=1).astype(BF16)
+                out[:, cols] = jnp.concatenate([nat[n, t, :rows] for t in range(chunk // 128)], axis=1).astype(BF16)
             else:
                 acc[:, cols] += part
             return 0
@@ -601,8 +601,8 @@
         pltpu.VMEM((2, rows, width), BF16),
         pltpu.VMEM((depth, features), BF16),
         pltpu.VMEM((rows, width), BF16),
-        *[pltpu.VMEM((heads, rows, HEAD_DIM), F32) for _ in range(3)],
-        pltpu.VMEM((features // 256, 2, rows, 128), F32),
+        *[pltpu.VMEM((heads, rows + sel_b // 4, HEAD_DIM), F32) for _ in range(3)],
+        pltpu.VMEM((features // 256, 2, rows + 8, 128), F32),
         pltpu.VMEM((heads, sel_b, three), BF16),
         pltpu.VMEM((heads, sel_c, three), BF16),
         pltpu.VMEM((heads, sel_b, three), BF16),

time: 53.5 us -> 53.5 us (level)
  no operation moved by 1% of the time
where the time goes in v4:
time: 53.5 us; the launch traced here: 53.3 us
  Pallas kernels  51 us (95%)
  local copies, waits for them, and re-layouts  2.31 us (4%)
    pallas_call x1, Pallas kernels, shards(): pl.pallas_call(kernel, out_shape=jax.ShapeDtypeStruct((rows, features), B...  51 us
    unnamed x5, local copies, waits for them, and re-layouts  2.31 us

profile of v4, /device:TPU:1, one launch (start us, length us, event | category | flops | bytes accessed | tf_op | source)
XLA Modules:
  0.0 53.3 jit_solution(14886793389854921433)
XLA Ops:
  0.0 0.0 copy-start
  0.0 0.7 %copy-done = s32[8,8]{1,0:T(8,128)S(1)} copy-done((s32[8,8]{1,0:T(8,128)S(1)}, s32[8,8]{1,0:T(8,128)}, u32[]{:S(2)}) %copy-start) | copy-done | bytes 280
  0.7 0.0 copy-start.1
  0.7 0.7 %copy-done.1 = s32[8]{0:T(128)S(1)} copy-done((s32[8]{0:T(128)S(1)}, s32[8]{0:T(128)}, u32[]{:S(2)}) %copy-start.1) | copy-done | bytes 56
  1.3 51.0 %shard_map.64 = bf16[512,1024]{1,0:T(8,128)(2,1)S(1)} custom-call(bf16[512,1024]{1,0:T(8,128)(2,1)} %q_hbm.1, bf16[512,1024]{1,0:T(8,128)(2,1)} %k_hbm.1, bf16[512,1024]{1,0:T(8,128)(2,1)} %v_hbm.1, s32[8,8]{1,0:T(8,128)S(1)} %copy-done, s32[1,8]{1,0:T(1,128)S(1)} %bitcast.1, bf16[4096,1024]{1,0:T(8,128)(2,1)} %w_hbm.1), custom_call_target="tpu_custom_call" | custom-call | tf_op jit(solution)/shard_map/pallas_call | solution.py:645
  52.4 1.0 %copy.8 = bf16[512,1024]{1,0:T(8,128)(2,1)} copy(bf16[512,1024]{1,0:T(8,128)(2,1)S(1)} %shard_map.64) | data formatting | bytes 2097152
Async XLA Ops:
  0.0 0.7 %copy-start = (s32[8,8]{1,0:T(8,128)S(1)}, s32[8,8]{1,0:T(8,128)}, u32[]{:S(2)}) copy-start(s32[8,8]{1,0:T(8,128)} %offs_b.1) | copy-start | bytes 772
  0.7 0.7 %copy-start.1 = (s32[8]{0:T(128)S(1)}, s32[8]{0:T(128)}, u32[]{:S(2)}) copy-start(s32[8]{0:T(128)} %param.10) | copy-start | bytes 100

commit v5 on v4

--- a/solution.py
+++ b/solution.py
@@ -543,10 +543,12 @@
         lax.fori_loop(0, width // chunk, columns, 0)
 
     project(0, xs, 0, heads, True)
-    for group in range(2):
-        forward(2, group)
-        project(1, from_left0 if group == 0 else from_left1, group * few, few, False)
-        project(3, from_right0 if group == 0 else from_right1, group * few, few, False)
+    forward(2, 0)
+    project(1, from_left0, 0, few, False)
+    forward(2, 1)
+    project(3, from_right0, 0, few, False)
+    project(1, from_left1, few, few, False)
+    project(3, from_right1, few, few, False)
     @pl.when(core == 0)
     def _():
         for n in range(mates):

time: 53.5 us -> 53.8 us (level)
  no operation moved by 1% of the time
where the time goes in v5:
time: 53.8 us; the launch traced here: 53.7 us
  Pallas kernels  51.3 us (95%)
  local copies, waits for them, and re-layouts  2.31 us (4%)
    pallas_call x1, Pallas kernels, shards(): pl.pallas_call(kernel, out_shape=jax.ShapeDtypeStruct((rows, features), B...  51.3 us
    unnamed x5, local copies, waits for them, and re-layouts  2.31 us

profile of v5, /device:TPU:1, one launch (start us, length us, event | category | flops | bytes accessed | tf_op | source)
XLA Modules:
  0.0 53.7 jit_solution(17581189924439557813)
XLA Ops:
  0.0 0.0 copy-start
  0.0 0.7 %copy-done = s32[8,8]{1,0:T(8,128)S(1)} copy-done((s32[8,8]{1,0:T(8,128)S(1)}, s32[8,8]{1,0:T(8,128)}, u32[]{:S(2)}) %copy-start) | copy-done | bytes 280
  0.7 0.0 copy-start.1
  0.7 0.7 %copy-done.1 = s32[8]{0:T(128)S(1)} copy-done((s32[8]{0:T(128)S(1)}, s32[8]{0:T(128)}, u32[]{:S(2)}) %copy-start.1) | copy-done | bytes 56
  1.3 51.3 %shard_map.64 = bf16[512,1024]{1,0:T(8,128)(2,1)S(1)} custom-call(bf16[512,1024]{1,0:T(8,128)(2,1)} %q_hbm.1, bf16[512,1024]{1,0:T(8,128)(2,1)} %k_hbm.1, bf16[512,1024]{1,0:T(8,128)(2,1)} %v_hbm.1, s32[8,8]{1,0:T(8,128)S(1)} %copy-done, s32[1,8]{1,0:T(1,128)S(1)} %bitcast.1, bf16[4096,1024]{1,0:T(8,128)(2,1)} %w_hbm.1), custom_call_target="tpu_custom_call" | custom-call | tf_op jit(solution)/shard_map/pallas_call | solution.py:647
  52.7 1.0 %copy.8 = bf16[512,1024]{1,0:T(8,128)(2,1)} copy(bf16[512,1024]{1,0:T(8,128)(2,1)S(1)} %shard_map.64) | data formatting | bytes 2097152
Async XLA Ops:
  0.0 0.7 %copy-start = (s32[8,8]{1,0:T(8,128)S(1)}, s32[8,8]{1,0:T(8,128)}, u32[]{:S(2)}) copy-start(s32[8,8]{1,0:T(8,128)} %offs_b.1) | copy-start | bytes 772
  0.7 0.7 %copy-start.1 = (s32[8]{0:T(128)S(1)}, s32[8]{0:T(128)}, u32[]{:S(2)}) copy-start(s32[8]{0:T(128)} %param.10) | copy-start | bytes 100
